TPU v7x, 32 devices: a whole 2x2x4 slice. The times are simulated.
32 devices in a mesh: seq: 16 (over z, y, core), tensor: 2 (over x).
Axes of the slice: x: 2, y: 2, z: 4, core: 2. Of those that a mesh axis runs over, the one named last changes fastest.
Arguments:
- tokens: bfloat16 [16384, 1024], P('seq'), may hold values from -6 to 6
- scene_lengths: int32 [4], replicated, may hold values from 1 to 7168, as said below
- w_query: bfloat16 [1, 1024, 1024], P(None, 'seq', 'tensor'), may hold values from -0.1875 to 0.1875
- w_key: bfloat16 [1, 1024, 1024], P(None, 'seq', 'tensor'), may hold values from -0.1875 to 0.1875
- w_value: bfloat16 [1, 1024, 1024], P(None, 'seq', 'tensor'), may hold values from -0.1875 to 0.1875
- w_out: bfloat16 [1, 1024, 1024], P(None, 'tensor', 'seq'), may hold values from -0.75 to 0.75
- w_up: bfloat16 [1, 1024, 4096], P(None, 'seq', 'tensor'), may hold values from -0.1875 to 0.1875
- w_down: bfloat16 [1, 4096, 1024], P(None, 'tensor', 'seq'), may hold values from -0.09375 to 0.09375
- norm_gain: bfloat16 [1, 2, 1024], P(None, None, 'seq'), may hold values from 0.099609375 to 1.8984375
- norm_bias: bfloat16 [1, 2, 1024], P(None, None, 'seq'), may hold values from -1.5 to 1.5
- cotangent: bfloat16 [16384, 1024], P('seq'), may hold values from -6 to 6
Outputs:
- activations: bfloat16 [16384, 1024], P('seq')
- grad_tokens: float32 [16384, 1024], P('seq')
- grad_query: float32 [1, 1024, 1024], P(None, 'seq', 'tensor')
- grad_key: float32 [1, 1024, 1024], P(None, 'seq', 'tensor')
- grad_value: float32 [1, 1024, 1024], P(None, 'seq', 'tensor')
- grad_out: float32 [1, 1024, 1024], P(None, 'tensor', 'seq')
- grad_up: float32 [1, 1024, 4096], P(None, 'seq', 'tensor')
- grad_down: float32 [1, 4096, 1024], P(None, 'tensor', 'seq')
- grad_gain: float32 [1, 2, 1024], P(None, None, 'seq')
- grad_bias: float32 [1, 2, 1024], P(None, None, 'seq')
Inputs may be any that keep to these rules, and one draw needn't show every extreme that they name: `scene_lengths`: the lengths sum to 16384. Exactly one scene, at a place drawn from the seed, has 7168 tokens; the others have fewer.
All inputs are finite; a program needn't handle non-finite values.
Results may differ from a plain program's by a relative error of at most 0.017.
Values may be sent and summed in bfloat16 or wider, within the bound.
A program may use at most 256 MiB of HBM per device.

v0:
```python
import functools

import jax
import jax.numpy as jnp
from jax import lax
from jax.experimental import pallas as pl
from jax.experimental.pallas import tpu as pltpu
from jax.sharding import PartitionSpec as P

HEAD_DIM = 64
BF = jnp.bfloat16
F32 = jnp.float32
norm_eps = 1e-06
neg_large = -1e30
log2_e = 1.4426950408889634
ln_2 = 0.6931471805599453
STAT_ROWS = 3
SAFE_BOUND = 60.0
PARTS = 2
VMEM_BYTES = 56 * 2**20


def dot(left, right, left_dim, right_dim):
    return lax.dot_general(
        left, right, (((left_dim,), (right_dim,)), ((), ())), preferred_element_type=F32
    )


def layer_norm(stream, gain_row, bias_row):
    centred = stream - jnp.mean(stream, axis=-1, keepdims=True)
    spread = jnp.mean(centred * centred, axis=-1, keepdims=True)
    return centred * lax.rsqrt(spread + norm_eps) * gain_row + bias_row


def gelu_tanh(value):
    return jax.nn.gelu(value, approximate=True)


def ring_of(devices):
    chips = devices // 2
    index = lax.axis_index("seq")
    core = lax.rem(index, 2)
    chip = index // 2
    if chips != 8:
        return chip, core, lambda place: 2 * place + core
    layer, column = chip // 2, lax.rem(chip, 2)
    place = layer + column * (7 - 2 * layer)

    def seq_index(place):
        side = place // 4
        depth = place + side * (7 - 2 * place)
        return depth * 4 + side * 2 + core

    return place, core, seq_index


def remote_copy(source, target, send_sem, recv_sem, seq):
    return pltpu.make_async_remote_copy(
        src_ref=source, dst_ref=target, send_sem=send_sem, recv_sem=recv_sem,
        device_id={"seq": seq}, device_id_type=pl.DeviceIdType.MESH,
    )


def meet(others):
    barrier = pltpu.get_barrier_semaphore()
    for other in others:
        pl.semaphore_signal(
            barrier, inc=1, device_id=other, device_id_type=pl.DeviceIdType.MESH
        )
    pl.semaphore_wait(barrier, len(others))


def project_kernel(
    tokens_ref, query_ref, key_ref, value_ref, gain_ref, bias_ref,
    sent_ref, normed_ref, weights_ref, norms_ref,
    gathered, scaled, send_right, recv_right, send_left, recv_left, send_peer, recv_peer,
    out_sem,
    *, devices, group, columns, width,
):
    chips = devices // 2
    depth = width // devices
    rows = tokens_ref.shape[0] // group
    place, core, seq_index = ring_of(devices)
    me = seq_index(place)
    right = seq_index(lax.rem(place + 1, chips))
    left = seq_index(lax.rem(place + chips - 1, chips))
    peer = me + 1 - 2 * core
    heads = columns // HEAD_DIM
    meet([{"seq": right}, {"seq": left}, {"seq": peer}])

    def slot(index):
        return gathered.at[pl.ds(pl.multiple_of(index * depth, depth), depth), :]

    mine = pl.ds(pl.multiple_of(me * depth, depth), depth)
    for which, ref in enumerate((query_ref, key_ref, value_ref)):
        gathered[mine, which * columns : (which + 1) * columns] = ref[0]
    norm_rows = jnp.concatenate(
        [gain_ref[0].astype(F32), bias_ref[0].astype(F32), jnp.zeros((124, depth), F32)], axis=0
    )
    gathered[mine, 3 * columns :] = norm_rows.T.astype(BF)

    to_right, to_left = chips // 2, chips - 1 - chips // 2

    def rightward(step):
        index = seq_index(lax.rem(place - step + chips, chips))
        return remote_copy(
            slot(index), slot(index), send_right.at[step], recv_right.at[step], right
        )

    def leftward(step):
        index = seq_index(lax.rem(place + step, chips))
        return remote_copy(slot(index), slot(index), send_left.at[step], recv_left.at[step], left)

    def across(distance):
        index = seq_index(lax.rem(place + distance + chips, chips))
        return remote_copy(
            slot(index), slot(index),
            send_peer.at[(distance + chips) % chips], recv_peer.at[(distance + chips) % chips], peer,
        )

    def arrive_right(step):
        index = seq_index(lax.rem(place - step - 1 + chips, chips))
        remote_copy(
            slot(index), slot(index), send_right.at[step], recv_right.at[step], right
        ).wait_recv()

    def arrive_left(step):
        index = seq_index(lax.rem(place + step + 1, chips))
        remote_copy(
            slot(index), slot(index), send_left.at[step], recv_left.at[step], left
        ).wait_recv()

    rightward(0).start()
    leftward(0).start()
    across(0).start()

    def normalize(index, carry):
        at = pl.ds(pl.multiple_of(index * 128, 128), 128)
        stream = tokens_ref[at, :].astype(F32)
        centred = stream - jnp.mean(stream, axis=-1, keepdims=True)
        spread = jnp.mean(centred * centred, axis=-1, keepdims=True)
        scaled[at, :] = centred * lax.rsqrt(spread + norm_eps)
        return carry

    lax.fori_loop(0, tokens_ref.shape[0] // 128, normalize, 0)

    for step in range(to_right):
        arrive_right(step)
        if step + 1 < to_right:
            rightward(step + 1).start()
        across(-step - 1).start()
        if step < to_left:
            arrive_left(step)
            if step + 1 < to_left:
                leftward(step + 1).start()
            across(step + 1).start()
    for distance in range(chips):
        index = seq_index(lax.rem(place + distance, chips)) + 1 - 2 * core
        remote_copy(
            slot(index), slot(index), send_peer.at[distance], recv_peer.at[distance], peer
        ).wait_recv()

    store = pltpu.make_async_copy(gathered.at[:, : 3 * columns], weights_ref, out_sem)
    store.start()
    norms = gathered[:, 3 * columns :].astype(F32).T
    norms_ref[...] = norms[0:8]

    def apply_norm(index, carry):
        at = pl.ds(pl.multiple_of(index * 128, 128), 128)
        normed_ref[at, :] = (scaled[at, :] * norms[0:1] + norms[2:3]).astype(BF)
        return carry

    lax.fori_loop(0, tokens_ref.shape[0] // 128, apply_norm, 0)
    for which in range(3):
        weights = gathered[:, which * columns : (which + 1) * columns].T
        factor = HEAD_DIM**-0.5 * log2_e if which == 0 else 1.0

        def project(core_index, carry, which=which, weights=weights, factor=factor):
            at = pl.ds(pl.multiple_of(core_index * rows, rows), rows)
            result = (dot(weights, normed_ref[at, :], 1, 1) * factor).astype(BF)
            for head in range(heads):
                sent_ref[head * group + core_index, which * HEAD_DIM : (which + 1) * HEAD_DIM, :] = (
                    result[head * HEAD_DIM : (head + 1) * HEAD_DIM, :]
                )
            return carry

        lax.fori_loop(0, group, project, 0)
    for step in range(to_right):
        rightward(step).wait_send()
    for step in range(to_left):
        leftward(step).wait_send()
    for distance in range(chips):
        across(distance).wait_send()
    store.wait()


def project(tokens, w_query, w_key, w_value, norm_gain, norm_bias, devices, group):
    own_rows, width = tokens.shape
    columns = w_query.shape[2]
    chips = devices // 2
    whole = pl.BlockSpec(memory_space=pltpu.VMEM)
    dma = pltpu.SemaphoreType.DMA
    return pl.pallas_call(
        functools.partial(
            project_kernel, devices=devices, group=group, columns=columns, width=width
        ),
        in_specs=[whole] * 6,
        out_specs=[whole, whole, pl.BlockSpec(memory_space=pl.ANY), whole],
        out_shape=[
            jax.ShapeDtypeStruct((devices, 3 * HEAD_DIM, own_rows // group), BF),
            jax.ShapeDtypeStruct((own_rows, width), BF),
            jax.ShapeDtypeStruct((width, 3 * columns), BF),
            jax.ShapeDtypeStruct((8, width), F32),
        ],
        scratch_shapes=[
            pltpu.VMEM((width, 3 * columns + 128), BF),
            pltpu.VMEM((own_rows, width), F32),
            dma((chips // 2,)), dma((chips // 2,)),
            dma((chips // 2,)), dma((chips // 2,)),
            dma((chips,)), dma((chips,)),
            dma,
        ],
        compiler_params=pltpu.CompilerParams(
            vmem_limit_bytes=VMEM_BYTES, collective_id=1, has_side_effects=True
        ),
        name="project",
    )(tokens, w_query, w_key, w_value, norm_gain, norm_bias)


def scene_span(ends_ref, scenes, first, last):
    low = jnp.int32(0)
    high = ends_ref[scenes - 1]
    for scene in range(scenes):
        low = jnp.where(first >= ends_ref[scene], ends_ref[scene], low)
    for scene in reversed(range(scenes)):
        high = jnp.where(last < ends_ref[scene], ends_ref[scene], high)
    return low, high


def scene_inside(ends_ref, scenes, row, position):
    start = jnp.zeros_like(row)
    end = jnp.zeros_like(row)
    before = jnp.int32(0)
    for scene in range(scenes):
        start = jnp.where(row == STAT_ROWS + scene, before, start)
        end = jnp.where(row == STAT_ROWS + scene, ends_ref[scene], end)
        before = ends_ref[scene]
    return (position >= start) & (position < end)


def key_extra(ends_ref, scenes, first, rows):
    row = lax.broadcasted_iota(jnp.int32, (64, rows), 0)
    position = first + lax.broadcasted_iota(jnp.int32, (64, rows), 1)
    inside = scene_inside(ends_ref, scenes, row, position)
    return jnp.where(row < STAT_ROWS, -1.0, jnp.where(inside, 1.0, 0.0)).astype(BF)


def query_extra(ends_ref, scenes, first, rows, stat):
    row = lax.broadcasted_iota(jnp.int32, (64, rows), 0)
    position = first + lax.broadcasted_iota(jnp.int32, (64, rows), 1)
    inside = scene_inside(ends_ref, scenes, row, position)
    is_scene = (row >= STAT_ROWS) & (row < STAT_ROWS + scenes)
    extra = jnp.where(is_scene & jnp.logical_not(inside), neg_large, 0.0)
    if stat is not None:
        extra = stat_rows(row, stat, extra)
    return extra.astype(BF)


def stat_rows(row, stat, extra):
    top = stat.astype(BF).astype(F32)
    middle = (stat - top).astype(BF).astype(F32)
    bottom = stat - top - middle
    extra = jnp.where(row == 0, top, extra)
    extra = jnp.where(row == 1, middle, extra)
    return jnp.where(row == 2, bottom, extra)


def walk_tiles(process, state, first, count, unit, sizes):
    at = first
    left = count
    for size in sizes:
        steps = left // size
        begin = at

        def step(index, carry, begin=begin, size=size):
            offset = pl.multiple_of((begin + index * size) * unit, unit)
            return process(offset, size * unit, carry)

        state = lax.fori_loop(0, steps, step, state)
        at = at + steps * size
        left = left - steps * size
    return state


def forward_kernel(
    ends_ref, me_ref, recv_ref, other_ref, out_ref, lse_ref, keys, values, key_top,
    *, scenes, group, total,
):
    block = pl.program_id(0)
    core = me_ref[0]
    sources = recv_ref.shape[0]
    rows = recv_ref.shape[2]

    @pl.when(block == 0)
    def _():
        values[64:80, :] = jnp.ones((16, total), BF)
        key_top[0] = 0.0
        for piece in range(group):
            place = core ^ piece

            def load(source, carry, piece=piece, place=place):
                first = pl.multiple_of((source * group + place) * rows, rows)
                if piece == 0:
                    key = recv_ref[source, 64:128, :]
                    value = recv_ref[source, 128:192, :]
                else:
                    key = other_ref[piece - 1, source, 0:64, :]
                    value = other_ref[piece - 1, source, 64:128, :]
                extra = key_extra(ends_ref, scenes, first, rows)
                keys[pl.ds(first, rows), :] = jnp.concatenate([key, extra], axis=0).T
                values[0:64, pl.ds(first, rows)] = value
                wide = key.astype(F32)
                key_top[0] = jnp.maximum(key_top[0], jnp.max(jnp.sum(wide * wide, axis=0)))
                return carry

            lax.fori_loop(0, sources, load, 0)

    first = (block * group + core) * rows
    low, high = scene_span(ends_ref, scenes, first, first + rows - 1)
    query = recv_ref[block, 0:64, :]
    wide = query.astype(F32)
    query_top = jnp.max(jnp.sum(wide * wide, axis=0))
    query = jnp.concatenate([query, query_extra(ends_ref, scenes, first, rows, None)], axis=0)
    unit = 256
    begin = low // unit
    count = (high + unit - 1) // unit - begin
    safe = query_top * key_top[0] <= SAFE_BOUND * SAFE_BOUND

    def scores_of(offset, size):
        return dot(keys[pl.ds(offset, size), :], query, 1, 0)

    def mix(offset, size, weights):
        return dot(values[:, pl.ds(offset, size)], weights.astype(BF), 1, 0)

    def write(total_mix, top):
        summed = total_mix[64:65, :]
        out_ref[0] = (total_mix[0:64, :] / summed).astype(BF)
        lse_ref[0] = top + jnp.log(summed) * log2_e

    @pl.when(safe)
    def _():
        def process(offset, size, carry):
            return carry + mix(offset, size, jnp.exp2(scores_of(offset, size)))

        write(
            walk_tiles(process, jnp.zeros((80, rows), F32), begin, count, unit, (8, 4, 2, 1)),
            0.0,
        )

    @pl.when(jnp.logical_not(safe))
    def _():
        def process(offset, size, carry):
            top, mixed = carry
            scores = scores_of(offset, size)
            new_top = jnp.maximum(top, jnp.max(scores, axis=0, keepdims=True))
            weights = jnp.exp2(scores - new_top)
            return new_top, mixed * jnp.exp2(top - new_top) + mix(offset, size, weights)

        start = (jnp.full((1, rows), neg_large, F32), jnp.zeros((80, rows), F32))
        top, mixed = walk_tiles(process, start, begin, count, unit, (1,))
        write(mixed, top)


def attention_forward(ends, me, recv, other, group):
    sources, _, rows = recv.shape
    total = sources * group * rows
    whole = pl.BlockSpec(memory_space=pltpu.VMEM)
    return pl.pallas_call(
        functools.partial(
            forward_kernel, scenes=ends.shape[0], group=group, total=total
        ),
        grid_spec=pltpu.PrefetchScalarGridSpec(
            num_scalar_prefetch=2,
            grid=(sources,),
            in_specs=[whole, whole],
            out_specs=[
                pl.BlockSpec((1, 64, rows), lambda b, *_: (b, 0, 0)),
                pl.BlockSpec((1, 1, rows), lambda b, *_: (b, 0, 0)),
            ],
            scratch_shapes=[
                pltpu.VMEM((total, 128), BF),
                pltpu.VMEM((80, total), BF),
                pltpu.SMEM((1,), F32),
            ],
        ),
        out_shape=[
            jax.ShapeDtypeStruct((sources, 64, rows), BF),
            jax.ShapeDtypeStruct((sources, 1, rows), F32),
        ],
        compiler_params=pltpu.CompilerParams(vmem_limit_bytes=VMEM_BYTES),
        cost_estimate=pl.CostEstimate(
            flops=60 * 10**9, bytes_accessed=8 * 10**6, transcendentals=45 * 10**6
        ),
        name="attention_forward",
    )(ends, me, recv, other)


def backward_kernel(ends_ref, me_ref, recv_ref, pieces_ref, *refs, scenes, group, parts):
    dout_refs = refs[:parts]
    out_ref, lse_ref, dquery_ref, dkeys_ref = refs[parts : parts + 4]
    queries, douts, queries_flat, douts_flat, dqueries = refs[parts + 4 :]
    block = pl.program_id(0)
    core = me_ref[0]
    sources = recv_ref.shape[0]
    rows = recv_ref.shape[2]
    span = group * rows

    @pl.when(block == 0)
    def _():
        dqueries[...] = jnp.zeros_like(dqueries)

        def load(source, carry):
            first = source * span + core * rows
            at = pl.ds(pl.multiple_of(source * rows, rows), rows)
            query = recv_ref[source, 0:64, :]
            dout = jnp.concatenate([ref[source] for ref in dout_refs], axis=1)
            delta = jnp.sum(
                dout.astype(F32) * out_ref[source].astype(F32), axis=0, keepdims=True
            )
            row = lax.broadcasted_iota(jnp.int32, (64, rows), 0)
            extra = query_extra(ends_ref, scenes, first, rows, lse_ref[source])
            queries[at, :] = jnp.concatenate([query, extra], axis=0).T
            extra = stat_rows(row, delta, jnp.zeros((64, rows), F32)).astype(BF)
            douts[at, :] = jnp.concatenate([dout, extra], axis=0).T
            queries_flat[:, at] = query
            douts_flat[:, at] = dout
            return carry

        lax.fori_loop(0, sources, load, 0)

    source = block // group
    place = block % group
    first = block * rows
    low, high = scene_span(ends_ref, scenes, first, first + rows - 1)
    extra = key_extra(ends_ref, scenes, first, rows)
    key = pieces_ref[0, 0, 0:64, :]
    key_wide = jnp.concatenate([key, extra], axis=0)
    value_wide = jnp.concatenate([pieces_ref[0, 0, 64:128, :], extra], axis=0)
    key_rows = key.T
    begin = (low - core * rows - rows + span) // span
    count = jnp.minimum((high - core * rows + span - 1) // span, sources) - begin

    def process(offset, size, carry):
        dkey, dvalue = carry
        at = pl.ds(offset, size)
        probs = jnp.exp2(dot(queries[at, :], key_wide, 1, 0))
        dprobs = dot(douts[at, :], value_wide, 1, 0)
        dscores = (probs * dprobs).astype(BF)
        dvalue = dvalue + dot(douts_flat[:, at], probs.astype(BF), 1, 0)
        dkey = dkey + dot(queries_flat[:, at], dscores, 1, 0)
        dqueries[at, :] += dot(dscores, key_rows, 1, 0)
        return dkey, dvalue

    zeros = jnp.zeros((64, rows), F32)
    dkey, dvalue = walk_tiles(process, (zeros, zeros), begin, count, rows, (4, 2, 1))
    dkeys_ref[0, 0, 0:64, :] = (dkey * ln_2).astype(BF)
    dkeys_ref[0, 0, 64:128, :] = dvalue.astype(BF)

    @pl.when(block == sources * group - 1)
    def _():
        def store(source, carry):
            at = pl.ds(pl.multiple_of(source * rows, rows), rows)
            dquery_ref[source] = (dqueries[at, :].T * HEAD_DIM**-0.5).astype(BF)
            return carry

        lax.fori_loop(0, sources, store, 0)


def attention_backward(ends, me, recv, pieces, dout, out, lse, group):
    sources, _, rows = recv.shape
    mine = sources * rows
    whole = pl.BlockSpec(memory_space=pltpu.VMEM)

    def piece_map(block, ends_ref, me_ref):
        return ((block % group) ^ me_ref[0], block // group, 0, 0)

    return pl.pallas_call(
        functools.partial(
            backward_kernel, scenes=ends.shape[0], group=group, parts=len(dout)
        ),
        grid_spec=pltpu.PrefetchScalarGridSpec(
            num_scalar_prefetch=2,
            grid=(sources * group,),
            in_specs=[whole, pl.BlockSpec((1, 1, 128, rows), piece_map)] + [whole] * (len(dout) + 2),
            out_specs=[whole, pl.BlockSpec((1, 1, 128, rows), piece_map)],
            scratch_shapes=[
                pltpu.VMEM((mine, 128), BF),
                pltpu.VMEM((mine, 128), BF),
                pltpu.VMEM((64, mine), BF),
                pltpu.VMEM((64, mine), BF),
                pltpu.VMEM((mine, 64), F32),
            ],
        ),
        out_shape=[
            jax.ShapeDtypeStruct((sources, 64, rows), BF),
            jax.ShapeDtypeStruct((group, sources, 128, rows), BF),
        ],
        compiler_params=pltpu.CompilerParams(vmem_limit_bytes=VMEM_BYTES),
        cost_estimate=pl.CostEstimate(
            flops=150 * 10**9, bytes_accessed=20 * 10**6, transcendentals=45 * 10**6
        ),
        name="attention_backward",
    )(ends, me, recv, pieces, *dout, out, lse)


def swap_tensor(part):
    return lax.ppermute(part, "tensor", [(0, 1), (1, 0)])


def sum_tensor(part):
    low = part.astype(BF)
    return low.astype(F32) + swap_tensor(low).astype(F32)


def per_device(
    tokens, scene_lengths, w_query, w_key, w_value, w_out, w_up, w_down,
    norm_gain, norm_bias, cotangent,
):
    own_rows, width = tokens.shape
    devices = lax.axis_size("seq")
    heads = w_query.shape[2] // HEAD_DIM
    columns = heads * HEAD_DIM
    hidden = w_up.shape[2]
    group = devices // heads
    rows = own_rows // group
    me = lax.rem(lax.axis_index("seq"), group).astype(jnp.int32).reshape(1)
    half = lax.axis_index("tensor")
    ends = jnp.cumsum(scene_lengths).astype(jnp.int32)

    def in_order(part):
        other = swap_tensor(part)
        return jnp.where(
            half == 0,
            jnp.concatenate([part, other], axis=-1),
            jnp.concatenate([other, part], axis=-1),
        )

    def to_owners(parts):
        return lax.all_to_all(parts, "seq", 0, 0, tiled=True)

    projected, normed_one, w_first, norms = project(
        tokens, w_query, w_key, w_value, norm_gain, norm_bias, devices, group
    )
    gains, biases = norms[0:2], norms[2:4]
    stream = tokens.astype(F32)
    out_part = in_order(w_out[0].T)
    second_part = jnp.concatenate([out_part, w_up[0], w_down[0].T], axis=1)
    recv = to_owners(projected)
    recv, second_part = lax.optimization_barrier((recv, second_part))
    second_all = lax.all_gather(second_part, "seq", axis=0, tiled=True)
    out_w = second_all[:, :width]
    out_own = lax.dynamic_slice_in_dim(out_w, half * columns, columns, 1)
    up_w = second_all[:, width : width + hidden]
    down_w = second_all[:, width + hidden :]
    own_piece = recv[:, HEAD_DIM:, :]

    def swap_core(part, by):
        return lax.ppermute(part, "seq", [(i, i ^ by) for i in range(devices)])

    others = jnp.stack([swap_core(own_piece, by) for by in range(1, group)])
    out_head, lse = attention_forward(ends, me, recv, others, group)

    part_rows = rows // PARTS

    def split(rows_all):
        cut = rows_all.reshape(group, PARTS, part_rows, rows_all.shape[1])
        return [cut[:, part].reshape(group * part_rows, -1) for part in range(PARTS)]

    def join(pieces_all):
        cut = [piece.reshape(group, part_rows, -1) for piece in pieces_all]
        return jnp.stack(cut, axis=1).reshape(own_rows, -1)

    mixed_parts, up_parts, mids, normed_parts, acts, dups, dys, dmids, douts = ([] for _ in range(9))
    dgain_two = dbias_two = 0.0
    dz_parts = split(cotangent)
    stream_parts = split(stream)
    for part in range(PARTS):
        piece = to_owners(out_head[:, :, part * part_rows : (part + 1) * part_rows])
        piece = piece.reshape(heads, group, HEAD_DIM, part_rows)
        mixed = piece.transpose(1, 3, 0, 2).reshape(group * part_rows, columns)
        mid = stream_parts[part] + dot(in_order(mixed), out_w, 1, 1)
        normed_raw, norm_two_back = jax.vjp(layer_norm, mid, gains[1], biases[1])
        normed_two = normed_raw.astype(BF)
        up_raw = dot(normed_two, up_w, 1, 0)
        act_raw, gelu_back = jax.vjp(gelu_tanh, up_raw)
        dz = dz_parts[part]
        dup = gelu_back(dot(dz, down_w, 1, 0))[0].astype(BF)
        dnormed_two = sum_tensor(dot(dup, up_w, 1, 1))
        dmid_norm, dgain, dbias = norm_two_back(dnormed_two)
        dgain_two, dbias_two = dgain_two + dgain, dbias_two + dbias
        dmid = dz.astype(F32) + dmid_norm
        dy = dmid.astype(BF)
        dout = dot(out_own, dy, 0, 1).astype(BF).reshape(heads, HEAD_DIM, group, part_rows)
        dout = dout.transpose(0, 2, 1, 3).reshape(devices, HEAD_DIM, part_rows)
        douts.append(to_owners(dout))
        mixed_parts.append(mixed)
        mids.append(mid)
        normed_parts.append(normed_two)
        acts.append(act_raw.astype(BF))
        dups.append(dup)
        dys.append(dy)
        dmids.append(dmid)
    dmid = join(dmids)
    act, dup_all, _ = lax.optimization_barrier((join(acts), join(dups), dout))
    last = join(mids) + sum_tensor(dot(act, down_w, 1, 1))
    grads_second = [
        dot(join(dys), join(mixed_parts), 0, 0),
        dot(join(normed_parts), dup_all, 0, 0),
        dot(cotangent, act, 0, 0),
    ]
    grads_second = [
        lax.psum_scatter(grad.astype(BF), "seq", scatter_dimension=0, tiled=True).astype(F32)
        for grad in grads_second
    ]

    pieces = jnp.concatenate([own_piece[None], others], axis=0)
    dquery, dpieces = attention_backward(ends, me, recv, pieces, douts, out_head, lse, group)
    dpiece = dpieces[0].astype(F32)
    for by in range(1, group):
        dpiece = dpiece + swap_core(dpieces[by], by).astype(F32)
    dheads = to_owners(jnp.concatenate([dquery, dpiece.astype(BF)], axis=1))
    dheads = dheads.reshape(heads, group, 3, HEAD_DIM, rows)
    dheads = dheads.transpose(1, 4, 2, 0, 3).reshape(own_rows, 3 * columns)

    dnormed_one = sum_tensor(dot(dheads, w_first, 1, 1))
    norm_one_back = jax.vjp(layer_norm, stream, gains[0], biases[0])[1]
    dstream_norm, dgain_one, dbias_one = norm_one_back(dnormed_one)
    dstream = dmid + dstream_norm
    grads_first = dot(normed_one, dheads, 0, 0).astype(BF)
    grads_first = lax.psum_scatter(grads_first, "seq", scatter_dimension=0, tiled=True)
    norm_grads = jnp.stack([dgain_one, dgain_two, dbias_one, dbias_two])
    norm_grads = norm_grads.reshape(4, devices, -1).transpose(1, 0, 2)
    norm_grads = jnp.sum(to_owners(norm_grads), axis=0)

    grads_first = grads_first.astype(F32).reshape(1, -1, 3, columns)
    return (
        last.astype(BF),
        dstream,
        grads_first[:, :, 0],
        grads_first[:, :, 1],
        grads_first[:, :, 2],
        grads_second[0].T[None],
        grads_second[1][None],
        grads_second[2].T[None],
        norm_grads[None, 0:2],
        norm_grads[None, 2:4],
    )


def solution(mesh):
    placed = (
        P("seq", None),
        P(),
        P(None, "seq", "tensor"),
        P(None, "seq", "tensor"),
        P(None, "seq", "tensor"),
        P(None, "tensor", "seq"),
        P(None, "seq", "tensor"),
        P(None, "tensor", "seq"),
        P(None, None, "seq"),
        P(None, None, "seq"),
        P("seq", None),
    )
    return jax.shard_map(
        per_device,
        mesh=mesh,
        in_specs=placed,
        out_specs=(
            P("seq", None),
            P("seq", None),
            P(None, "seq", "tensor"),
            P(None, "seq", "tensor"),
            P(None, "seq", "tensor"),
            P(None, "tensor", "seq"),
            P(None, "seq", "tensor"),
            P(None, "tensor", "seq"),
            P(None, None, "seq"),
            P(None, None, "seq"),
        ),
        check_vma=False,
    )
```

profile of v0, /device:TPU:0, one launch (start us, length us, event | category | flops | bytes accessed | tf_op | source)
XLA Modules:
  0.0 714.3 jit_solution(6362992189835339593)
XLA Ops:
  7.2 38.0 %project.1 = (bf16[16,192,512]{2,1,0:T(8,128)(2,1)}, bf16[1024,1024]{1,0:T(8,128)(2,1)}, bf16[1024,1536]{1,0:T(8,128)(2,1)}, f32[8,1024]{1,0:T(8,128)}) custom-call(bf16[1024,1024]{1,0:T(8,128)(2,1)} %tokens_ref.1, bf16[1,64,512]{2,1,0:T(8,128)(2,1)} %query_ref.1, bf16[1,64,512]{2,1,0:T(8,128)(2,1)} %key_ref.1, bf16[1,64,512]{2,1,0:T(8,128)(2,1)} %value_ref.1, ...), custom_call_target="tpu_custom_call" | custom-call | tf_op jit(solution)/shard_map/project/pallas_call | solution.py:203
  55.8 52.6 %all-to-all-done.recv_ref = bf16[16,192,512]{2,1,0:T(8,128)(2,1)S(1)} async-done(((bf16[16,192,512]{2,1,0:T(8,128)(2,1)}), bf16[16,192,512]{2,1,0:T(8,128)(2,1)S(1)}, u32[]{:S(2)}, u32[]{:S(2)}) %all-to-all-start) | async-done | bytes 3145760 | tf_op jit(solution)/shard_map/all_to_all | solution.py:549
  117.4 64.2 %attention_forward.1 = (bf16[16,64,512]{2,1,0:T(8,128)(2,1)}, f32[16,1,512]{2,1,0:T(1,128)}) custom-call(s32[4]{0:T(128)} %bitcast.231, s32[1]{0:T(128)} %bitcast.4.me_ref, bf16[16,192,512]{2,1,0:T(8,128)(2,1)} %copy-done.5, bf16[1,16,128,512]{3,2,1,0:T(8,128)(2,1)} %bitcast.212), custom_call_target="tpu_custom_call" | custom-call | flops 60000002048 | bytes 8000000 | tf_op jit(solution)/shard_map/attention_forward/pallas_call | solution.py:378
  183.9 30.7 %all_to_all.35 = bf16[16,64,256]{2,1,0:T(8,128)(2,1)S(1)} all-to-all(bf16[16,64,256]{2,1,0:T(8,128)(2,1)S(1)} %get-tuple-element.89), channel_id=1, replica_groups=mesh['seq'=16,'tensor'=2] {'seq'}, dimensions={0} | all-to-all | bytes 1048576 | tf_op jit(solution)/shard_map/all_to_all | solution.py:549
  214.5 5.5 all-to-all-start.2
  226.2 8.3 %all-to-all-done.2 = bf16[16,64,256]{2,1,0:T(8,128)(2,1)S(1)} async-done(((bf16[16,64,256]{2,1,0:T(8,128)(2,1)}), bf16[16,64,256]{2,1,0:T(8,128)(2,1)S(1)}, u32[]{:S(2)}, u32[]{:S(2)}) %all-to-all-start.2) | async-done | bytes 524320 | tf_op jit(solution)/shard_map/all_to_all | solution.py:549
  239.7 4.4 fusion.94
  244.1 6.0 collective-permute-done.3
  254.6 4.5 multiply_convert_fusion
  259.1 5.0 fusion.13
  269.0 4.5 multiply_convert_fusion.1
  273.5 4.6 fusion.6
  282.1 4.6 pad_maximum_fusion.4.pieces_ref
  294.0 20.6 %collective-permute-done.6 = bf16[512,1024]{1,0:T(8,128)(2,1)} collective-permute-done((bf16[512,1024]{1,0:T(8,128)(2,1)}, bf16[512,1024]{1,0:T(8,128)(2,1)}, u32[]{:S(2)}, u32[]{:S(2)}) %collective-permute-start.6) | collective-permute-done | bytes 1048608 | tf_op jit(solution)/shard_map/ppermute | solution.py:517
  318.8 4.5 fusion.87
  330.5 5.0 all-to-all-start.3
  351.5 6.0 all-to-all-start.4
  361.7 6.2 convert_bitcast_fusion
  368.0 6.5 copy.94
  375.3 140.4 %attention_backward.1 = (bf16[16,64,512]{2,1,0:T(8,128)(2,1)}, bf16[2,16,128,512]{3,2,1,0:T(8,128)(2,1)}) custom-call(s32[4]{0:T(128)} %bitcast.232, s32[1]{0:T(128)} %bitcast.4.me_ref, bf16[16,192,512]{2,1,0:T(8,128)(2,1)} %copy-done.5, bf16[2,16,128,512]{3,2,1,0:T(8,128)(2,1)} %pad_maximum_fusion.4.pieces_ref, ...), custom_call_target="tpu_custom_call" | custom-call | flops 149999992832 | bytes 20000000 | tf_op jit(solution)/shard_map/attention_backward/pallas_call | solution.py:487
  524.4 6.2 all-to-all-start.5
  532.9 6.3 convolution_convert_fusion.1
  541.1 9.3 %fusion.45 = bf16[1024,1024]{1,0:T(8,128)(2,1)} fusion(bf16[1024,2048]{1,0:T(8,128)(2,1)} %bitcast.195, bf16[1024,5120]{1,0:T(8,128)(2,1)} %all-gather.2.cloned.1.call-done), kind=kOutput, calls=%fused_computation.88 | convolution fusion | flops 4296015872 | bytes 10485760 | tf_op jit(solution)/shard_map/dot_general | solution.py:24
  551.9 55.0 %all-to-all-done.5 = bf16[16,192,512]{2,1,0:T(8,128)(2,1)} async-done(((bf16[16,192,512]{2,1,0:T(8,128)(2,1)}), bf16[16,192,512]{2,1,0:T(8,128)(2,1)}, u32[]{:S(2)}, u32[]{:S(2)}) %all-to-all-start.5) | async-done | bytes 3145760 | tf_op jit(solution)/shard_map/all_to_all | solution.py:549
  606.9 5.2 copy.80
  614.0 4.9 convolution_convert_fusion.2
  620.3 5.0 convolution_convert_fusion
  636.8 5.9 fusion.21
  648.7 18.8 %collective-permute-done.8 = bf16[1024,1024]{1,0:T(8,128)(2,1)} collective-permute-done((bf16[1024,1024]{1,0:T(8,128)(2,1)}, bf16[1024,1024]{1,0:T(8,128)(2,1)}, u32[]{:S(2)}, u32[]{:S(2)}) %collective-permute-start.8) | collective-permute-done | bytes 2097184 | tf_op jit(solution)/shard_map/ppermute | solution.py:517
  671.3 4.3 multiply_reduce_fusion
  676.5 16.9 %all-to-all-start.6 = ((f32[16,1,256]{2,1,0:T(1,128)}), f32[16,1,256]{2,1,0:T(1,128)S(1)}, u32[]{:S(2)}, u32[]{:S(2)}) async-start(f32[16,1,256]{2,1,0:T(1,128)} %reshape.270), calls=%async_computation.9 | async-start | bytes 32768 | tf_op jit(solution)/shard_map/all_to_all | solution.py:549
  693.4 5.8 bitcast_add_fusion
  (201 shorter events, 134.0 us)
Async XLA Ops:
  45.2 8.7 %copy-start.32 = (bf16[1,2048,64]{1,2,0:T(8,128)(2,1)S(1)}, bf16[1,2048,64]{1,2,0:T(8,128)(2,1)}, u32[]{:S(2)}) copy-start(bf16[1,2048,64]{1,2,0:T(8,128)(2,1)} %param.18) | copy-start | bytes 786436
  45.2 63.2 %all-to-all-start = ((bf16[16,192,512]{2,1,0:T(8,128)(2,1)}), bf16[16,192,512]{2,1,0:T(8,128)(2,1)S(1)}, u32[]{:S(2)}, u32[]{:S(2)}) async-start(bf16[16,192,512]{2,1,0:T(8,128)(2,1)} %get-tuple-element.22), calls=%async_computation | async-start | bytes 6291456 | tf_op jit(solution)/shard_map/all_to_all | solution.py:549
  49.1 189.8 %all-gather.2.cloned.1.call-start = ((), (), s32[]{:S(2)}) async-start(), calls=%async_computation.11 | async-start | bytes 11141120 | tf_op jit(solution)/shard_map/all_gather | solution.py:560
  49.1 4.7 collective-permute-start
  111.3 4.8 collective-permute-start.1
  181.6 38.5 %copy-start = (bf16[1024,1024]{1,0:T(8,128)(2,1)S(1)}, bf16[1024,1024]{1,0:T(8,128)(2,1)}, u32[]{:S(2)}) copy-start(bf16[1024,1024]{1,0:T(8,128)(2,1)} %tokens_ref.1) | copy-start | bytes 6291460
  214.5 20.0 %all-to-all-start.2 = ((bf16[16,64,256]{2,1,0:T(8,128)(2,1)}), bf16[16,64,256]{2,1,0:T(8,128)(2,1)S(1)}, u32[]{:S(2)}, u32[]{:S(2)}) async-start(bf16[16,64,256]{2,1,0:T(8,128)(2,1)} %get-tuple-element.90), calls=%async_computation.2 | async-start | bytes 1048576 | tf_op jit(solution)/shard_map/all_to_all | solution.py:549
  223.1 12.8 %copy-start.30 = (bf16[64,8,2,256]{3,1,2,0:T(8,128)(2,1)}, bf16[64,8,2,256]{3,1,2,0:T(8,128)(2,1)S(1)}, u32[]{:S(2)}) copy-start(bf16[64,8,2,256]{3,1,2,0:T(8,128)(2,1)S(1)} %copy.100) | copy-start | bytes 1572868
  223.1 15.7 %collective-permute-start.2 = (bf16[512,512]{0,1:T(8,128)(2,1)S(1)}, bf16[512,512]{0,1:T(8,128)(2,1)S(1)}, u32[]{:S(2)}, u32[]{:S(2)}) collective-permute-start(bf16[512,512]{0,1:T(8,128)(2,1)S(1)} %bitcast.217), channel_id=1, source_target_pairs={{0,1},{1,0},{2,3},{3,2},{4,5},{5,4},{6,7},{7,6},{8,9},{9,8},{10,11... | collective-permute-start | bytes 1572872 | tf_op jit(solution)/shard_map/ppermute | solution.py:517
  235.9 14.2 %collective-permute-start.3 = (bf16[512,512]{0,1:T(8,128)(2,1)}, bf16[512,512]{0,1:T(8,128)(2,1)}, u32[]{:S(2)}, u32[]{:S(2)}) collective-permute-start(bf16[512,512]{0,1:T(8,128)(2,1)} %bitcast.111), channel_id=1, source_target_pairs={{0,1},{1,0},{2,3},{3,2},{4,5},{5,4},{6,7},{7,6},{8,9},{9,8},{10,11... | collective-permute-start | bytes 1572872 | tf_op jit(solution)/shard_map/ppermute | solution.py:517
  239.7 10.4 %copy-start.27 = (f32[2,1,256,1024]{3,2,1,0:T(8,128)S(1)}, f32[2,1,256,1024]{3,2,1,0:T(8,128)}, u32[]{:S(2)}) copy-start(f32[2,1,256,1024]{3,2,1,0:T(8,128)} %get-tuple-element.88) | copy-start | bytes 6291460
  239.7 10.4 %copy-start.31 = (bf16[1024,5120]{1,0:T(8,128)(2,1)S(1)}, bf16[1024,5120]{1,0:T(8,128)(2,1)}, u32[]{:S(2)}) copy-start(bf16[1024,5120]{1,0:T(8,128)(2,1)} %all-gather.2.cloned.1.call-done) | copy-start | bytes 31457284
  244.1 74.7 %copy-start.2 = (f32[512,1024]{1,0:T(8,128)}, f32[512,1024]{1,0:T(8,128)S(1)}, u32[]{:S(2)}) copy-start(f32[512,1024]{1,0:T(8,128)S(1)} %get-tuple-element.109) | copy-start | bytes 6291460
  254.6 14.4 %copy-start.11 = (bf16[512,1024]{1,0:T(8,128)(2,1)}, bf16[512,1024]{1,0:T(8,128)(2,1)S(1)}, u32[]{:S(2)}) copy-start(bf16[512,1024]{1,0:T(8,128)(2,1)S(1)} %get-tuple-element.97) | copy-start | bytes 3145732
  267.6 26.4 %collective-permute-start.4 = (bf16[512,1024]{1,0:T(8,128)(2,1)}, bf16[512,1024]{1,0:T(8,128)(2,1)}, u32[]{:S(2)}, u32[]{:S(2)}) collective-permute-start(bf16[512,1024]{1,0:T(8,128)(2,1)} %fusion.52), channel_id=1, source_target_pairs={{0,1},{1,0},{2,3},{3,2},{4,5},{5,4},{6,7},{7,6},{8,9},{9,8},{10,11... | collective-permute-start | bytes 3145736 | tf_op jit(solution)/shard_map/ppermute | solution.py:517
  281.6 33.0 %collective-permute-start.6 = (bf16[512,1024]{1,0:T(8,128)(2,1)}, bf16[512,1024]{1,0:T(8,128)(2,1)}, u32[]{:S(2)}, u32[]{:S(2)}) collective-permute-start(bf16[512,1024]{1,0:T(8,128)(2,1)} %fusion.55), channel_id=1, source_target_pairs={{0,1},{1,0},{2,3},{3,2},{4,5},{5,4},{6,7},{7,6},{8,9},{9,8},{10,11... | collective-permute-start | bytes 3145736 | tf_op jit(solution)/shard_map/ppermute | solution.py:517
  290.7 23.9 %copy-start.4 = (f32[512,1024]{1,0:T(8,128)S(1)}, f32[512,1024]{1,0:T(8,128)}, u32[]{:S(2)}) copy-start(f32[512,1024]{1,0:T(8,128)} %copy-done.3) | copy-start | bytes 6291460
  292.6 32.5 %copy-start.20 = (bf16[1024,1024]{1,0:T(8,128)(2,1)}, bf16[1024,1024]{1,0:T(8,128)(2,1)S(1)}, u32[]{:S(2)}) copy-start(bf16[1024,1024]{1,0:T(8,128)(2,1)S(1)} %slice.88) | copy-start | bytes 6291460
  325.1 10.6 %copy-start.6 = (f32[512,1024]{1,0:T(8,128)S(1)}, f32[512,1024]{1,0:T(8,128)}, u32[]{:S(2)}) copy-start(f32[512,1024]{1,0:T(8,128)} %get-tuple-element.102) | copy-start | bytes 6291460
  330.5 21.0 %all-to-all-start.3 = ((bf16[16,64,256]{2,1,0:T(8,128)(2,1)}), bf16[16,64,256]{2,1,0:T(8,128)(2,1)}, u32[]{:S(2)}, u32[]{:S(2)}) async-start(bf16[16,64,256]{2,1,0:T(8,128)(2,1)} %bitcast.206), calls=%async_computation.3 | async-start | bytes 1048576 | tf_op jit(solution)/shard_map/all_to_all | solution.py:549
  335.6 299.7 %reduce-scatter.9.cloned.1.call-start = ((), (), s32[]{:S(2)}) async-start(), calls=%async_computation.13 | async-start | bytes 1114112 | tf_op jit(solution)/shard_map/reduce_scatter | solution.py:622
  349.7 7.8 %copy-start.22 = (bf16[512,2048]{1,0:T(8,128)(2,1)S(1)}, bf16[512,2048]{1,0:T(8,128)(2,1)}, u32[]{:S(2)}) copy-start(bf16[512,2048]{1,0:T(8,128)(2,1)} %get-tuple-element.112) | copy-start | bytes 6291460
  351.5 23.0 %all-to-all-start.4 = ((bf16[16,64,256]{2,1,0:T(8,128)(2,1)}), bf16[16,64,256]{2,1,0:T(8,128)(2,1)S(1)}, u32[]{:S(2)}, u32[]{:S(2)}) async-start(bf16[16,64,256]{2,1,0:T(8,128)(2,1)} %bitcast.40), calls=%async_computation.4 | async-start | bytes 1048576 | tf_op jit(solution)/shard_map/all_to_all | solution.py:549
  357.5 285.2 %reduce-scatter.13.cloned.1.call-start = ((), (), s32[]{:S(2)}) async-start(), calls=%async_computation.15 | async-start | bytes 4456448
  517.6 4.2 collective-permute-start.7
  524.4 82.5 %all-to-all-start.5 = ((bf16[16,192,512]{2,1,0:T(8,128)(2,1)}), bf16[16,192,512]{2,1,0:T(8,128)(2,1)}, u32[]{:S(2)}, u32[]{:S(2)}) async-start(bf16[16,192,512]{2,1,0:T(8,128)(2,1)} %pad_maximum_fusion.5), calls=%async_computation.5 | async-start | bytes 6291456 | tf_op jit(solution)/shard_map/all_to_all | solution.py:549
  530.6 116.3 %reduce-scatter.11.cloned.1.call-start = ((), (), s32[]{:S(2)}) async-start(), calls=%async_computation.14 | async-start | bytes 4456448 | tf_op jit(solution)/shard_map/reduce_scatter | solution.py:622
  539.1 164.9 %reduce-scatter.7.cloned.1.call-start = ((), (), s32[]{:S(2)}) async-start(), calls=%async_computation.12 | async-start | bytes 3342336 | tf_op jit(solution)/shard_map/reduce_scatter | solution.py:640
  550.4 86.4 %collective-permute-start.5 = (bf16[1024,1024]{1,0:T(8,128)(2,1)}, bf16[1024,1024]{1,0:T(8,128)(2,1)}, u32[]{:S(2)}, u32[]{:S(2)}) collective-permute-start(bf16[1024,1024]{1,0:T(8,128)(2,1)} %fusion.45), channel_id=1, source_target_pairs={{0,1},{1,0},{2,3},{3,2},{4,5},{5,4},{6,7},{7,6},{8,9},{9,8},{10,11... | collective-permute-start | bytes 6291464 | tf_op jit(solution)/shard_map/ppermute | solution.py:517
  618.9 48.6 %collective-permute-start.8 = (bf16[1024,1024]{1,0:T(8,128)(2,1)}, bf16[1024,1024]{1,0:T(8,128)(2,1)}, u32[]{:S(2)}, u32[]{:S(2)}) collective-permute-start(bf16[1024,1024]{1,0:T(8,128)(2,1)} %convolution_convert_fusion.2), channel_id=1, source_target_pairs={{0,1},{1,0},{2,3},{3,2},{4,5},{5,4},{6,7},{7,6},{8,9},{9,8},{10,11... | collective-permute-start | bytes 6291464 | tf_op jit(solution)/shard_map/ppermute | solution.py:517
  642.7 24.8 %copy-start.34 = (f32[1,1024]{1,0:T(1,128)S(1)}, f32[1,1024]{1,0:T(1,128)}, u32[]{:S(2)}) copy-start(f32[1,1024]{1,0:T(1,128)} %get-tuple-element.94) | copy-start | bytes 12292
  676.5 23.5 %all-to-all-start.6 = ((f32[16,1,256]{2,1,0:T(1,128)}), f32[16,1,256]{2,1,0:T(1,128)S(1)}, u32[]{:S(2)}, u32[]{:S(2)}) async-start(f32[16,1,256]{2,1,0:T(1,128)} %reshape.270), calls=%async_computation.9 | async-start | bytes 32768 | tf_op jit(solution)/shard_map/all_to_all | solution.py:549
  (31 other events, 105.8 us)
Sparse Core Ops, SparseCore 0:
  108.5 102.8 all-gather.1
  345.7 58.6 reduce-scatter.8
  408.7 71.6 reduce-scatter.12
  539.3 90.7 reduce-scatter.10
  634.2 69.7 reduce-scatter.6
where the time goes:
time: 718 us; the launch traced here: 714 us
  Pallas kernels  243 us (34%)
  waiting for transfers between devices  176 us (25%)
  matrix products  70.7 us (10%)
  local copies, waits for them, and re-layouts  63.2 us (9%)
  other arithmetic  61.8 us (9%)
  starting transfers between devices  54.5 us (8%)
  blocking collectives  30.7 us (4%)
  between operations  14.6 us (2%)
    pallas_call x1, Pallas kernels, attention_backward(): pl.pallas_call(functools.partial(backward_kernel, scenes=ends.shape[0], g...  140 us
    all_to_all x6, waiting for transfers between devices, to_owners(): return lax.all_to_all(parts, 'seq', 0, 0, tiled=True)  117 us
    dot_general x16, matrix products, dot(): lax.dot_general(left, right, (((left_dim,), (right_dim,)), ((), ())), pre...  70.7 us
    pallas_call x1, Pallas kernels, attention_forward(): pl.pallas_call(functools.partial(forward_kernel, scenes=ends.shape[0], gr...  64.2 us
    ppermute x7, waiting for transfers between devices, swap_tensor(): return lax.ppermute(part, 'tensor', [(0, 1), (1, 0)])  50 us
    all_to_all x6, starting transfers between devices, to_owners(): return lax.all_to_all(parts, 'seq', 0, 0, tiled=True)  43.5 us
    pallas_call x1, Pallas kernels, project(): pl.pallas_call(functools.partial(project_kernel, devices=devices, group=g...  38 us
    all_to_all x1, blocking collectives, to_owners(): return lax.all_to_all(parts, 'seq', 0, 0, tiled=True)  30.7 us
  transfers between devices with their start and end apart: 20, of which 12 were waited for; matrix products, arithmetic and copies ran while one was open for 21% of the time, Pallas kernels for 29%

commit v1 on v0

--- a/solution.py
+++ b/solution.py
@@ -16,7 +16,6 @@
 ln_2 = 0.6931471805599453
 STAT_ROWS = 3
 SAFE_BOUND = 60.0
-PARTS = 2
 VMEM_BYTES = 56 * 2**20
 
 
@@ -24,16 +23,6 @@
     return lax.dot_general(
         left, right, (((left_dim,), (right_dim,)), ((), ())), preferred_element_type=F32
     )
-
-
-def layer_norm(stream, gain_row, bias_row):
-    centred = stream - jnp.mean(stream, axis=-1, keepdims=True)
-    spread = jnp.mean(centred * centred, axis=-1, keepdims=True)
-    return centred * lax.rsqrt(spread + norm_eps) * gain_row + bias_row
-
-
-def gelu_tanh(value):
-    return jax.nn.gelu(value, approximate=True)
 
 
 def ring_of(devices):
@@ -227,6 +216,546 @@
     )(tokens, w_query, w_key, w_value, norm_gain, norm_bias)
 
 
+def finish_kernel(
+    dheads_ref, normed_ref, weights_ref, tokens_ref, dmid_ref, norms_ref, second_ref,
+    dstream_ref, dquery_ref, dkey_ref, dvalue_ref, dgain_ref, dbias_ref,
+    flat, partial_sent, partial_got, partial, from_peer, first_right, first_left,
+    ring_right, ring_left, total, few_sent, few_got,
+    x_send, x_recv, peer_send, peer_recv, right_send, right_recv, left_send, left_recv,
+    few_send, few_recv,
+    *, devices, group, columns, width,
+):
+    chips = devices // 2
+    depth = width // devices
+    own_rows = tokens_ref.shape[0]
+    rows = own_rows // group
+    heads = columns // HEAD_DIM
+    wide = 3 * columns + 128
+    cut = first_right.shape[1]
+    place, core, seq_index = ring_of(devices)
+    me = seq_index(place)
+    right = {"seq": seq_index(lax.rem(place + 1, chips))}
+    left = {"seq": seq_index(lax.rem(place + chips - 1, chips))}
+    peer = {"seq": me + 1 - 2 * core}
+    across = {"tensor": 1 - lax.axis_index("tensor")}
+    meet([right, left, peer, across])
+
+    def copy_to(source, target, send_sem, recv_sem, where):
+        return pltpu.make_async_remote_copy(
+            src_ref=source, dst_ref=target, send_sem=send_sem, recv_sem=recv_sem,
+            device_id=where, device_id_type=pl.DeviceIdType.MESH,
+        )
+
+    def flatten(index, carry):
+        head = index // group
+        part = lax.rem(index, group)
+        at = pl.ds(pl.multiple_of(part * rows, rows), rows)
+        for which in range(3):
+            to = pl.ds(
+                pl.multiple_of(which * columns + head * HEAD_DIM, HEAD_DIM), HEAD_DIM
+            )
+            flat[to, at] = dheads_ref[index, which * HEAD_DIM : (which + 1) * HEAD_DIM, :]
+        return carry
+
+    lax.fori_loop(0, devices, flatten, 0)
+
+    parts = 4
+    part_rows = own_rows // parts
+
+    def x_copy(part):
+        at = pl.ds(part * part_rows, part_rows)
+        return copy_to(
+            partial_sent.at[at, :], partial_got.at[at, :], x_send.at[part], x_recv.at[part], across
+        )
+
+    def unit_rows(at):
+        stream = tokens_ref[at, :].astype(F32)
+        centred = stream - jnp.mean(stream, axis=-1, keepdims=True)
+        spread = jnp.mean(centred * centred, axis=-1, keepdims=True)
+        inverse = lax.rsqrt(spread + norm_eps)
+        return centred * inverse, inverse
+
+    gain_sum = jnp.zeros((1, width), F32)
+    bias_sum = jnp.zeros((1, width), F32)
+    for part in range(parts):
+        at = pl.ds(part * part_rows, part_rows)
+        result = dot(flat[:, at].T, weights_ref[...], 1, 1)
+        partial_sent[at, :] = result.astype(BF)
+        x_copy(part).start()
+        unit, _ = unit_rows(at)
+        gain_sum = gain_sum + jnp.sum(result * unit, axis=0, keepdims=True)
+        bias_sum = bias_sum + jnp.sum(result, axis=0, keepdims=True)
+
+    lines = 256
+    for line in range(width // lines):
+        at = slice(line * lines, (line + 1) * lines)
+        partial[at, 0 : 3 * columns] = dot(normed_ref[:, at].T, flat[...], 1, 1).astype(BF)
+    norm_rows = jnp.concatenate(
+        [
+            gain_sum, second_ref[0:1, :] * 0.5, bias_sum, second_ref[1:2, :] * 0.5,
+            jnp.zeros((124, width), F32),
+        ],
+        axis=0,
+    )
+    partial[:, 3 * columns :] = norm_rows.T.astype(BF)
+
+    order = []
+    for step in range(chips // 2):
+        for offset in (-step - 1, step + 1):
+            if offset % chips not in order:
+                order.append(offset % chips)
+    order.append(0)
+
+    def peer_copy(number):
+        where = lax.rem(place + order[number], chips)
+        theirs = seq_index(where) + 1 - 2 * core
+        return copy_to(
+            partial.at[pl.ds(pl.multiple_of(theirs * depth, depth), depth), :],
+            from_peer.at[pl.ds(pl.multiple_of(where * depth, depth), depth), :],
+            peer_send.at[number], peer_recv.at[number], peer,
+        )
+
+    for number in range(chips):
+        peer_copy(number).start()
+
+    waited = []
+
+    def chip_block(offset, low, high):
+        number = order.index(offset % chips)
+        if number not in waited:
+            peer_copy(number).wait_recv()
+            waited.append(number)
+        where = lax.rem(place + offset % chips, chips)
+        own = pl.ds(pl.multiple_of(seq_index(where) * depth, depth), depth)
+        got = pl.ds(pl.multiple_of(where * depth, depth), depth)
+        return partial[own, low:high].astype(F32) + from_peer[got, low:high].astype(F32)
+
+    def finish_norm(part):
+        x_copy(part).wait_recv()
+
+        def piece(index, carry):
+            at = pl.ds(pl.multiple_of(part * part_rows + index * 128, 128), 128)
+            dnormed = partial_sent[at, :].astype(F32) + partial_got[at, :].astype(F32)
+            unit, inverse = unit_rows(at)
+            dunit = dnormed * norms_ref[0:1, :]
+            mean = jnp.mean(dunit, axis=-1, keepdims=True)
+            along = jnp.mean(dunit * unit, axis=-1, keepdims=True)
+            dstream_ref[at, :] = dmid_ref[at, :] + (dunit - mean - unit * along) * inverse
+            return carry
+
+        lax.fori_loop(0, part_rows // 128, piece, 0)
+
+    steps = chips - 1
+
+    def ring_copy(step, toward_right):
+        if toward_right:
+            source = first_right if step == 0 else ring_right.at[step - 1]
+            return copy_to(
+                source, ring_right.at[step], right_send.at[step], right_recv.at[step], right
+            )
+        source = first_left if step == 0 else ring_left.at[step - 1]
+        return copy_to(source, ring_left.at[step], left_send.at[step], left_recv.at[step], left)
+
+    first_right[...] = chip_block(-1, 0, cut).astype(BF)
+    ring_copy(0, True).start()
+    first_left[...] = chip_block(1, cut, wide).astype(BF)
+    ring_copy(0, False).start()
+    for step in range(steps):
+        if step in (0, steps // 2, steps - 1):
+            finish_norm((0, steps // 2, steps - 1).index(step))
+        for toward_right, ring, low, high in (
+            (True, ring_right, 0, cut), (False, ring_left, cut, wide),
+        ):
+            ring_copy(step, toward_right).wait_recv()
+            offset = -step - 2 if toward_right else step + 2
+            summed = ring[step].astype(F32) + chip_block(offset, low, high)
+            if step + 1 < steps:
+                ring[step] = summed.astype(BF)
+                ring_copy(step + 1, toward_right).start()
+            else:
+                total[:, low:high] = summed
+    few_sent[...] = total[:, 3 * columns :]
+    few = copy_to(few_sent, few_got, few_send, few_recv, across)
+    few.start()
+    dquery_ref[0] = total[:, 0:columns]
+    dkey_ref[0] = total[:, columns : 2 * columns]
+    dvalue_ref[0] = total[:, 2 * columns : 3 * columns]
+    finish_norm(3)
+    few.wait()
+    norm_rows = (few_sent[...] + few_got[...]).T
+    dgain_ref[0] = norm_rows[0:2, :]
+    dbias_ref[0] = norm_rows[2:4, :]
+    for part in range(parts):
+        x_copy(part).wait_send()
+    for number in range(chips):
+        peer_copy(number).wait_send()
+    for step in range(steps):
+        ring_copy(step, True).wait_send()
+        ring_copy(step, False).wait_send()
+
+
+def finish(dheads, normed, weights, tokens, dmid, norms, second, devices, group):
+    own_rows, width = tokens.shape
+    columns = weights.shape[1] // 3
+    chips = devices // 2
+    depth = width // devices
+    wide = 3 * columns + 128
+    cut = (wide // 128 + 1) // 2 * 128
+    steps = chips - 1
+    whole = pl.BlockSpec(memory_space=pltpu.VMEM)
+    dma = pltpu.SemaphoreType.DMA
+    return pl.pallas_call(
+        functools.partial(
+            finish_kernel, devices=devices, group=group, columns=columns, width=width
+        ),
+        in_specs=[whole] * 7,
+        out_specs=[whole] * 6,
+        out_shape=[jax.ShapeDtypeStruct((own_rows, width), F32)]
+        + [jax.ShapeDtypeStruct((1, depth, columns), F32)] * 3
+        + [jax.ShapeDtypeStruct((1, 2, depth), F32)] * 2,
+        scratch_shapes=[
+            pltpu.VMEM((3 * columns, own_rows), BF),
+            pltpu.VMEM((own_rows, width), BF),
+            pltpu.VMEM((own_rows, width), BF),
+            pltpu.VMEM((width, wide), BF),
+            pltpu.VMEM((chips * depth, wide), BF),
+            pltpu.VMEM((depth, cut), BF),
+            pltpu.VMEM((depth, wide - cut), BF),
+            pltpu.VMEM((steps, depth, cut), BF),
+            pltpu.VMEM((steps, depth, wide - cut), BF),
+            pltpu.VMEM((depth, wide), F32),
+            pltpu.VMEM((depth, 128), F32),
+            pltpu.VMEM((depth, 128), F32),
+            dma((4,)), dma((4,)),
+            dma((chips,)), dma((chips,)),
+            dma((steps,)), dma((steps,)),
+            dma((steps,)), dma((steps,)),
+            dma, dma,
+        ],
+        compiler_params=pltpu.CompilerParams(
+            vmem_limit_bytes=VMEM_BYTES, collective_id=2, has_side_effects=True
+        ),
+        name="finish",
+    )(dheads, normed, weights, tokens, dmid, norms, second)
+
+
+def middle_kernel(
+    mixed_ref, tokens_ref, dz_ref, second_ref, norms_ref,
+    dout_ref, dmid_ref, mid_ref, z_ref, grads_ref, norm_grads_ref,
+    weights, tokens, dz, flat, flat_other, normed, act, dup, mid, dmid, dsent, dgot, dy, z,
+    out_t, dout, stage,
+    load_sem, flat_send, flat_recv, x_send, x_recv, head_send, head_recv, store_sem, stage_sem,
+    *, devices, group, columns, hidden,
+):
+    own_rows, width = tokens.shape
+    rows = own_rows // group
+    heads = columns // HEAD_DIM
+    parts = x_send.shape[0]
+    part_rows = own_rows // parts
+    block = 512
+    me = lax.axis_index("seq").astype(jnp.int32)
+    core = lax.rem(me, group)
+    half = lax.axis_index("tensor").astype(jnp.int32)
+    across = {"tensor": 1 - half}
+
+    loads = [
+        pltpu.make_async_copy(second_ref.at[:, 0:width], weights.at[:, 0:width], load_sem.at[0]),
+        pltpu.make_async_copy(tokens_ref, tokens, load_sem.at[1]),
+        pltpu.make_async_copy(second_ref.at[:, width:], weights.at[:, width:], load_sem.at[2]),
+        pltpu.make_async_copy(dz_ref, dz, load_sem.at[3]),
+    ]
+    for load in loads:
+        load.start()
+
+    barrier = pltpu.get_barrier_semaphore()
+    for other in range(devices):
+        @pl.when(me != other)
+        def _(other=other):
+            pl.semaphore_signal(
+                barrier, inc=1, device_id={"seq": other}, device_id_type=pl.DeviceIdType.MESH
+            )
+
+    pl.semaphore_signal(
+        barrier, inc=1, device_id=across, device_id_type=pl.DeviceIdType.MESH
+    )
+    pl.semaphore_wait(barrier, devices)
+
+    def copy_to(source, target, send_sem, recv_sem, where):
+        return pltpu.make_async_remote_copy(
+            src_ref=source, dst_ref=target, send_sem=send_sem, recv_sem=recv_sem,
+            device_id=where, device_id_type=pl.DeviceIdType.MESH,
+        )
+
+    def rows_of(part):
+        return pl.ds(pl.multiple_of(part * part_rows, part_rows), part_rows)
+
+    def flatten(index, carry):
+        head = index // group
+        at = pl.ds(pl.multiple_of(lax.rem(index, group) * rows, rows), rows)
+        flat[pl.ds(pl.multiple_of(head * HEAD_DIM, HEAD_DIM), HEAD_DIM), at] = mixed_ref[index]
+        return carry
+
+    lax.fori_loop(0, devices, flatten, 0)
+
+    def flat_copy(part):
+        at = rows_of(part)
+        return copy_to(
+            flat.at[:, at], flat_other.at[:, at], flat_send.at[part], flat_recv.at[part], across
+        )
+
+    def x_copy(part):
+        at = rows_of(part)
+        return copy_to(dsent.at[at, :], dgot.at[at, :], x_send.at[part], x_recv.at[part], across)
+
+    for part in range(parts):
+        flat_copy(part).start()
+    loads[0].wait()
+    out_t[...] = weights[:, pl.ds(pl.multiple_of(half * columns, columns), columns)].T
+    for load in loads[1:]:
+        load.wait()
+    first_half = half == 0
+
+    def unit_rows(at):
+        stream = mid[at, :]
+        centred = stream - jnp.mean(stream, axis=-1, keepdims=True)
+        spread = jnp.mean(centred * centred, axis=-1, keepdims=True)
+        inverse = lax.rsqrt(spread + norm_eps)
+        return centred * inverse, inverse
+
+    def store_mid(part):
+        at = rows_of(part)
+        return pltpu.make_async_copy(mid.at[at, :], mid_ref.at[at, :], store_sem.at[0, part])
+
+    def forward(part, carry):
+        at = rows_of(part)
+        flat_copy(part).wait_recv()
+        own, other = flat[:, at], flat_other[:, at]
+        low = jnp.where(first_half, own, other).T
+        high = jnp.where(first_half, other, own).T
+        projected = dot(low, weights[:, 0:columns], 1, 1) + dot(
+            high, weights[:, columns:width], 1, 1
+        )
+        mid[at, :] = tokens[at, :].astype(F32) + projected
+        store_mid(part).start()
+        unit, _ = unit_rows(at)
+        normed[at, :] = (unit * norms_ref[1:2, :] + norms_ref[3:4, :]).astype(BF)
+
+        def hidden_block(index, total):
+            cut = pl.ds(pl.multiple_of(index * block, block), block)
+            up_cut = pl.ds(pl.multiple_of(width + index * block, block), block)
+            down_cut = pl.ds(pl.multiple_of(width + hidden + index * block, block), block)
+            up_w = weights[:, up_cut]
+            up = dot(normed[at, :], up_w, 1, 0)
+            dact = dot(dz[at, :], weights[:, down_cut], 1, 0)
+            square = up * up
+            bend = jnp.tanh(0.7978845608028654 * up * (1.0 + 0.044715 * square))
+            grow = 0.5 + 0.5 * bend
+            slope = grow + 0.5 * up * (1.0 - bend * bend) * (
+                0.7978845608028654 + 0.10703222440890037 * square
+            )
+            act[at, cut] = (up * grow).astype(BF)
+            dup_block = (dact * slope).astype(BF)
+            dup[at, cut] = dup_block
+            return total + dot(dup_block, up_w, 1, 1)
+
+        total = lax.fori_loop(
+            0, hidden // block, hidden_block, jnp.zeros((part_rows, width), F32)
+        )
+        dsent[at, :] = total.astype(BF)
+        x_copy(part).start()
+        return carry
+
+    lax.fori_loop(0, parts, forward, 0)
+
+    piece_rows = min(part_rows, rows)
+    pieces = rows // piece_rows
+
+    def head_copies(piece, head):
+        start = piece * piece_rows
+        owner = head * group + start // rows
+        slot = lax.rem(piece, pieces)
+        source = dout.at[
+            pl.ds(pl.multiple_of(head * HEAD_DIM, HEAD_DIM), HEAD_DIM),
+            pl.ds(pl.multiple_of(start, piece_rows), piece_rows),
+        ]
+        target = dout_ref.at[me, :, pl.ds(pl.multiple_of(slot * piece_rows, piece_rows), piece_rows)]
+        away = copy_to(
+            source, target, head_send.at[head, piece], head_recv.at[me, slot], {"seq": owner}
+        )
+        home = pltpu.make_async_copy(source, target, head_send.at[head, piece])
+        return away, home, owner == me
+
+    def send_heads(part):
+        def send(index, carry):
+            piece = part * (part_rows // piece_rows) + index // heads
+            away, home, is_home = head_copies(piece, lax.rem(index, heads))
+
+            @pl.when(is_home)
+            def _():
+                home.start()
+
+            @pl.when(jnp.logical_not(is_home))
+            def _():
+                away.start()
+
+            return carry
+
+        lax.fori_loop(0, heads * (part_rows // piece_rows), send, 0)
+
+    def store_dmid(part):
+        at = rows_of(part)
+        return pltpu.make_async_copy(dmid.at[at, :], dmid_ref.at[at, :], store_sem.at[1, part])
+
+    def backward(part, sums):
+        gain_sum, bias_sum = sums
+        at = rows_of(part)
+        x_copy(part).wait_recv()
+        dnormed = dsent[at, :].astype(F32) + dgot[at, :].astype(F32)
+        unit, inverse = unit_rows(at)
+        dunit = dnormed * norms_ref[1:2, :]
+        mean = jnp.mean(dunit, axis=-1, keepdims=True)
+        along = jnp.mean(dunit * unit, axis=-1, keepdims=True)
+        result = dz[at, :].astype(F32) + (dunit - mean - unit * along) * inverse
+        dmid[at, :] = result
+        store_dmid(part).start()
+        low = result.astype(BF)
+        dy[at, :] = low
+        dout[:, at] = dot(out_t[...], low, 1, 1).astype(BF)
+        send_heads(part)
+        gain_sum = gain_sum + jnp.sum(dnormed * unit, axis=0, keepdims=True)
+        bias_sum = bias_sum + jnp.sum(dnormed, axis=0, keepdims=True)
+        return gain_sum, bias_sum
+
+    def last_product(part, carry):
+        at = rows_of(part)
+        z[at, :] = dot(act[at, :], weights[:, width + hidden :], 1, 1).astype(BF)
+        return carry
+
+    lax.fori_loop(0, parts, last_product, 0)
+    store_z = pltpu.make_async_copy(z, z_ref, load_sem.at[0])
+    store_z.start()
+
+    def grads_into(left_t, right_ref, first_column):
+        blocks = right_ref.shape[1] // block
+
+        def store(index, slot):
+            cut = pl.ds(pl.multiple_of(first_column + index * block, block), block)
+            return pltpu.make_async_copy(stage.at[slot], grads_ref.at[:, cut], stage_sem.at[slot])
+
+        def one(index, carry):
+            slot = lax.rem(index, 2)
+
+            @pl.when(index >= 2)
+            def _():
+                store(index - 2, slot).wait()
+
+            cut = pl.ds(pl.multiple_of(index * block, block), block)
+            stage[slot] = dot(left_t, right_ref[:, cut], 1, 0).astype(BF)
+            store(index, slot).start()
+            return carry
+
+        lax.fori_loop(0, blocks, one, 0)
+        for index in range(blocks - 2, blocks):
+            store(index, index % 2).wait()
+
+    sums = (jnp.zeros((1, width), F32), jnp.zeros((1, width), F32))
+    sums = backward(0, sums)
+    grads_into(normed[...].T, dup, columns)
+    sums = backward(1, sums)
+    grads_into(dz[...].T, act, columns + hidden)
+    for part in range(2, parts):
+        sums = backward(part, sums)
+    stage[0] = dot(dy[...].T, flat[...], 1, 1).astype(BF)
+    store_out = pltpu.make_async_copy(stage.at[0], grads_ref.at[:, 0:columns], stage_sem.at[0])
+    store_out.start()
+    norm_grads_ref[...] = jnp.concatenate([*sums, jnp.zeros((6, width), F32)], axis=0)
+
+    def wait_sent(index, carry):
+        away, home, is_home = head_copies(index // heads, lax.rem(index, heads))
+
+        @pl.when(is_home)
+        def _():
+            home.wait()
+
+        @pl.when(jnp.logical_not(is_home))
+        def _():
+            away.wait_send()
+
+        return carry
+
+    lax.fori_loop(0, heads * (own_rows // piece_rows), wait_sent, 0)
+
+    def wait_heads(index, carry):
+        source = index // pieces
+        slot = lax.rem(index, pieces)
+        cut = pl.ds(pl.multiple_of(slot * piece_rows, piece_rows), piece_rows)
+
+        @pl.when(source != me)
+        def _():
+            copy_to(
+                dout.at[0:HEAD_DIM, 0:piece_rows], dout_ref.at[source, :, cut],
+                head_send.at[0, 0], head_recv.at[source, slot], {"seq": source},
+            ).wait_recv()
+
+        return carry
+
+    lax.fori_loop(0, devices * pieces, wait_heads, 0)
+    for part in range(parts):
+        flat_copy(part).wait_send()
+        x_copy(part).wait_send()
+        store_mid(part).wait()
+        store_dmid(part).wait()
+    store_z.wait()
+    store_out.wait()
+
+
+def middle(mixed, tokens, dz, second, norms, devices, group, columns):
+    own_rows, width = tokens.shape
+    rows = own_rows // group
+    hidden = (second.shape[1] - width) // 2
+    parts = 4
+    piece_rows = min(own_rows // parts, rows)
+    whole = pl.BlockSpec(memory_space=pltpu.VMEM)
+    far = pl.BlockSpec(memory_space=pl.ANY)
+    dma = pltpu.SemaphoreType.DMA
+    vmem = pltpu.VMEM
+    return pl.pallas_call(
+        functools.partial(
+            middle_kernel, devices=devices, group=group, columns=columns, hidden=hidden
+        ),
+        in_specs=[whole, far, far, far, whole],
+        out_specs=[far] * 5 + [whole],
+        out_shape=[
+            jax.ShapeDtypeStruct((devices, HEAD_DIM, rows), BF),
+            jax.ShapeDtypeStruct((own_rows, width), F32),
+            jax.ShapeDtypeStruct((own_rows, width), F32),
+            jax.ShapeDtypeStruct((own_rows, width), BF),
+            jax.ShapeDtypeStruct((width, columns + 2 * hidden), BF),
+            jax.ShapeDtypeStruct((8, width), F32),
+        ],
+        scratch_shapes=[
+            vmem((width, width + 2 * hidden), BF),
+            vmem((own_rows, width), BF), vmem((own_rows, width), BF),
+            vmem((columns, own_rows), BF), vmem((columns, own_rows), BF),
+            vmem((own_rows, width), BF),
+            vmem((own_rows, hidden), BF), vmem((own_rows, hidden), BF),
+            vmem((own_rows, width), F32), vmem((own_rows, width), F32),
+            vmem((own_rows, width), BF), vmem((own_rows, width), BF),
+            vmem((own_rows, width), BF), vmem((own_rows, width), BF),
+            vmem((columns, width), BF), vmem((columns, own_rows), BF),
+            vmem((2, width, 512), BF),
+            dma((4,)), dma((parts,)), dma((parts,)), dma((parts,)), dma((parts,)),
+            dma((columns // HEAD_DIM, own_rows // piece_rows)),
+            dma((devices, rows // piece_rows)),
+            dma((2, parts)), dma((2,)),
+        ],
+        compiler_params=pltpu.CompilerParams(
+            vmem_limit_bytes=60 * 2**20, collective_id=3, has_side_effects=True
+        ),
+        name="middle",
+    )(mixed, tokens, dz, second, norms)
+
+
 def scene_span(ends_ref, scenes, first, last):
     low = jnp.int32(0)
     high = ends_ref[scenes - 1]
@@ -517,11 +1046,6 @@
     return lax.ppermute(part, "tensor", [(0, 1), (1, 0)])
 
 
-def sum_tensor(part):
-    low = part.astype(BF)
-    return low.astype(F32) + swap_tensor(low).astype(F32)
-
-
 def per_device(
     tokens, scene_lengths, w_query, w_key, w_value, w_out, w_up, w_down,
     norm_gain, norm_bias, cotangent,
@@ -551,17 +1075,11 @@
     projected, normed_one, w_first, norms = project(
         tokens, w_query, w_key, w_value, norm_gain, norm_bias, devices, group
     )
-    gains, biases = norms[0:2], norms[2:4]
-    stream = tokens.astype(F32)
     out_part = in_order(w_out[0].T)
     second_part = jnp.concatenate([out_part, w_up[0], w_down[0].T], axis=1)
     recv = to_owners(projected)
     recv, second_part = lax.optimization_barrier((recv, second_part))
     second_all = lax.all_gather(second_part, "seq", axis=0, tiled=True)
-    out_w = second_all[:, :width]
-    out_own = lax.dynamic_slice_in_dim(out_w, half * columns, columns, 1)
-    up_w = second_all[:, width : width + hidden]
-    down_w = second_all[:, width + hidden :]
     own_piece = recv[:, HEAD_DIM:, :]
 
     def swap_core(part, by):
@@ -570,90 +1088,35 @@
     others = jnp.stack([swap_core(own_piece, by) for by in range(1, group)])
     out_head, lse = attention_forward(ends, me, recv, others, group)
 
-    part_rows = rows // PARTS
-
-    def split(rows_all):
-        cut = rows_all.reshape(group, PARTS, part_rows, rows_all.shape[1])
-        return [cut[:, part].reshape(group * part_rows, -1) for part in range(PARTS)]
-
-    def join(pieces_all):
-        cut = [piece.reshape(group, part_rows, -1) for piece in pieces_all]
-        return jnp.stack(cut, axis=1).reshape(own_rows, -1)
-
-    mixed_parts, up_parts, mids, normed_parts, acts, dups, dys, dmids, douts = ([] for _ in range(9))
-    dgain_two = dbias_two = 0.0
-    dz_parts = split(cotangent)
-    stream_parts = split(stream)
-    for part in range(PARTS):
-        piece = to_owners(out_head[:, :, part * part_rows : (part + 1) * part_rows])
-        piece = piece.reshape(heads, group, HEAD_DIM, part_rows)
-        mixed = piece.transpose(1, 3, 0, 2).reshape(group * part_rows, columns)
-        mid = stream_parts[part] + dot(in_order(mixed), out_w, 1, 1)
-        normed_raw, norm_two_back = jax.vjp(layer_norm, mid, gains[1], biases[1])
-        normed_two = normed_raw.astype(BF)
-        up_raw = dot(normed_two, up_w, 1, 0)
-        act_raw, gelu_back = jax.vjp(gelu_tanh, up_raw)
-        dz = dz_parts[part]
-        dup = gelu_back(dot(dz, down_w, 1, 0))[0].astype(BF)
-        dnormed_two = sum_tensor(dot(dup, up_w, 1, 1))
-        dmid_norm, dgain, dbias = norm_two_back(dnormed_two)
-        dgain_two, dbias_two = dgain_two + dgain, dbias_two + dbias
-        dmid = dz.astype(F32) + dmid_norm
-        dy = dmid.astype(BF)
-        dout = dot(out_own, dy, 0, 1).astype(BF).reshape(heads, HEAD_DIM, group, part_rows)
-        dout = dout.transpose(0, 2, 1, 3).reshape(devices, HEAD_DIM, part_rows)
-        douts.append(to_owners(dout))
-        mixed_parts.append(mixed)
-        mids.append(mid)
-        normed_parts.append(normed_two)
-        acts.append(act_raw.astype(BF))
-        dups.append(dup)
-        dys.append(dy)
-        dmids.append(dmid)
-    dmid = join(dmids)
-    act, dup_all, _ = lax.optimization_barrier((join(acts), join(dups), dout))
-    last = join(mids) + sum_tensor(dot(act, down_w, 1, 1))
-    grads_second = [
-        dot(join(dys), join(mixed_parts), 0, 0),
-        dot(join(normed_parts), dup_all, 0, 0),
-        dot(cotangent, act, 0, 0),
-    ]
-    grads_second = [
-        lax.psum_scatter(grad.astype(BF), "seq", scatter_dimension=0, tiled=True).astype(F32)
-        for grad in grads_second
-    ]
+    dout, dmid, mid, z, grads_second, second_norms = middle(
+        to_owners(out_head), tokens, cotangent, second_all, norms, devices, group, columns
+    )
+    grads_second = lax.psum_scatter(grads_second, "seq", scatter_dimension=0, tiled=True)
+    grads_second = grads_second.astype(F32)
 
     pieces = jnp.concatenate([own_piece[None], others], axis=0)
-    dquery, dpieces = attention_backward(ends, me, recv, pieces, douts, out_head, lse, group)
+    dquery, dpieces = attention_backward(ends, me, recv, pieces, [dout], out_head, lse, group)
     dpiece = dpieces[0].astype(F32)
     for by in range(1, group):
         dpiece = dpiece + swap_core(dpieces[by], by).astype(F32)
-    dheads = to_owners(jnp.concatenate([dquery, dpiece.astype(BF)], axis=1))
-    dheads = dheads.reshape(heads, group, 3, HEAD_DIM, rows)
-    dheads = dheads.transpose(1, 4, 2, 0, 3).reshape(own_rows, 3 * columns)
-
-    dnormed_one = sum_tensor(dot(dheads, w_first, 1, 1))
-    norm_one_back = jax.vjp(layer_norm, stream, gains[0], biases[0])[1]
-    dstream_norm, dgain_one, dbias_one = norm_one_back(dnormed_one)
-    dstream = dmid + dstream_norm
-    grads_first = dot(normed_one, dheads, 0, 0).astype(BF)
-    grads_first = lax.psum_scatter(grads_first, "seq", scatter_dimension=0, tiled=True)
-    norm_grads = jnp.stack([dgain_one, dgain_two, dbias_one, dbias_two])
-    norm_grads = norm_grads.reshape(4, devices, -1).transpose(1, 0, 2)
-    norm_grads = jnp.sum(to_owners(norm_grads), axis=0)
-
-    grads_first = grads_first.astype(F32).reshape(1, -1, 3, columns)
+    dsent = jnp.concatenate([dquery, dpiece.astype(BF)], axis=1)
+    z, dsent = lax.optimization_barrier((z, dsent))
+    dheads = to_owners(dsent)
+    last = mid + (z.astype(F32) + swap_tensor(z).astype(F32))
+    dstream, dquery_w, dkey_w, dvalue_w, dgain, dbias = finish(
+        dheads, normed_one, w_first, tokens, dmid, norms, second_norms, devices, group
+    )
     return (
         last.astype(BF),
         dstream,
-        grads_first[:, :, 0],
-        grads_first[:, :, 1],
-        grads_first[:, :, 2],
-        grads_second[0].T[None],
-        grads_second[1][None],
-        grads_second[2].T[None],
-        norm_grads[None, 0:2],
-        norm_grads[None, 2:4],
+        dquery_w,
+        dkey_w,
+        dvalue_w,
+        grads_second[:, :columns].T[None],
+        grads_second[:, columns : columns + hidden][None],
+        grads_second[:, columns + hidden :].T[None],
+        dgain,
+        dbias,
     )
 
 

time: 718 us -> 609 us (0.85)
  Pallas kernels: 243 us -> 388 us
  matrix products: 70.7 us -> 0 us
  other arithmetic: 61.8 us -> 15.7 us
  local copies, waits for them, and re-layouts: 63.2 us -> 18.1 us
  waiting for transfers between devices: 176 us -> 145 us
  blocking collectives: 30.7 us -> 0 us
  starting transfers between devices: 54.5 us -> 26.1 us
    pallas_call x0 -> x2, Pallas kernels: none -> 165 us  [the longest x1 98.2 us: middle(): pl.pallas_call(functools.partial(middle_kernel, devices=devices, group=gr...]
    dot_general x16 -> x0, matrix products: 70.7 us -> none  [dot(): lax.dot_general(left, right, (((left_dim,), (right_dim,)), ((), ())), pre...]
    all_to_all x1 -> x0, blocking collectives: 30.7 us -> none  [to_owners(): return lax.all_to_all(parts, 'seq', 0, 0, tiled=True)]
    all_to_all x6 -> x3, waiting for transfers between devices: 117 us -> 86.5 us  [to_owners(): return lax.all_to_all(parts, 'seq', 0, 0, tiled=True)]
    all_to_all x6 -> x3, starting transfers between devices: 43.5 us -> 23 us  [to_owners(): return lax.all_to_all(parts, 'seq', 0, 0, tiled=True)]
    reduce_sum x8 -> x0, other arithmetic: 17.9 us -> none  [the longest x2 8.49 us: layer_norm(): return centred * lax.rsqrt(spread + norm_eps) * gain_row + bias_row]
    pallas_call x1, Pallas kernels: 140 us -> 126 us  [attention_backward(): pl.pallas_call(functools.partial(backward_kernel, scenes=ends.shape[0], g...]
    reshape x8 -> x0, local copies, waits for them, and re-layouts: 12.2 us -> none  [the longest x1 5.18 us: per_device(): dheads = dheads.reshape(heads, group, 3, HEAD_DIM, rows)]
  transfers between devices with their start and end apart: 20 -> 9, of which waited for: 12 -> 8; matrix products, arithmetic and copies ran while one was open for 21% -> 3% of each run, Pallas kernels for 29% -> 41%
where the time goes in v1:
time: 609 us; the launch traced here: 607 us
  Pallas kernels  388 us (64%)
  waiting for transfers between devices  145 us (24%)
  starting transfers between devices  26.1 us (4%)
  local copies, waits for them, and re-layouts  18.1 us (3%)
  other arithmetic  15.7 us (3%)
  between operations  14.4 us (2%)
    pallas_call x1, Pallas kernels, attention_backward(): pl.pallas_call(functools.partial(backward_kernel, scenes=ends.shape[0], g...  126 us
    pallas_call x1, Pallas kernels, middle(): pl.pallas_call(functools.partial(middle_kernel, devices=devices, group=gr...  98.2 us
    all_to_all x3, waiting for transfers between devices, to_owners(): return lax.all_to_all(parts, 'seq', 0, 0, tiled=True)  86.5 us
    pallas_call x1, Pallas kernels, finish(): pl.pallas_call(functools.partial(finish_kernel, devices=devices, group=gr...  67.1 us
    pallas_call x1, Pallas kernels, attention_forward(): pl.pallas_call(functools.partial(forward_kernel, scenes=ends.shape[0], gr...  58.5 us
    ppermute x2, waiting for transfers between devices, swap_tensor(): return lax.ppermute(part, 'tensor', [(0, 1), (1, 0)])  50.6 us
    pallas_call x1, Pallas kernels, project(): pl.pallas_call(functools.partial(project_kernel, devices=devices, group=g...  37.9 us
    all_to_all x3, starting transfers between devices, to_owners(): return lax.all_to_all(parts, 'seq', 0, 0, tiled=True)  23 us
  transfers between devices with their start and end apart: 9, of which 8 were waited for; matrix products, arithmetic and copies ran while one was open for 3% of the time, Pallas kernels for 41%

profile of v1, /device:TPU:0, one launch (start us, length us, event | category | flops | bytes accessed | tf_op | source)
XLA Modules:
  0.0 607.0 jit_solution(16027114157665107937)
XLA Ops:
  7.2 37.9 %project.1 = (bf16[16,192,512]{2,1,0:T(8,128)(2,1)}, bf16[1024,1024]{1,0:T(8,128)(2,1)}, bf16[1024,1536]{1,0:T(8,128)(2,1)}, f32[8,1024]{1,0:T(8,128)}) custom-call(bf16[1024,1024]{1,0:T(8,128)(2,1)} %tokens_ref.5, bf16[1,64,512]{2,1,0:T(8,128)(2,1)} %query_ref.1, bf16[1,64,512]{2,1,0:T(8,128)(2,1)} %key_ref.1, bf16[1,64,512]{2,1,0:T(8,128)(2,1)} %value_ref.1, ...), custom_call_target="tpu_custom_call" | custom-call | tf_op jit(solution)/shard_map/project/pallas_call | solution.py:192
  45.2 3.9 all-to-all-start
  49.1 1.6 collective-permute-start
  50.7 3.2 collective-permute-done
  53.9 1.9 pad_maximum_fusion.2
  55.8 52.6 %all-to-all-done.recv_ref = bf16[16,192,512]{2,1,0:T(8,128)(2,1)S(1)} async-done(((bf16[16,192,512]{2,1,0:T(8,128)(2,1)}), bf16[16,192,512]{2,1,0:T(8,128)(2,1)S(1)}, u32[]{:S(2)}, u32[]{:S(2)}) %all-to-all-start) | async-done | bytes 3145760 | tf_op jit(solution)/shard_map/all_to_all | solution.py:1073
  108.4 2.7 slice_bitcast_fusion.4
  111.2 0.8 collective-permute-start.1
  112.0 0.7 reduce-window.9
  112.7 3.3 collective-permute-done.1
  116.0 1.4 copy-done.5
  117.4 58.5 %attention_forward.1 = (bf16[16,64,512]{2,1,0:T(8,128)(2,1)}, f32[16,1,512]{2,1,0:T(1,128)}) custom-call(s32[4]{0:T(128)} %bitcast.35, s32[1]{0:T(128)} %bitcast.2.me_ref, bf16[16,192,512]{2,1,0:T(8,128)(2,1)} %copy-done.1, bf16[1,16,128,512]{3,2,1,0:T(8,128)(2,1)} %bitcast.28), custom_call_target="tpu_custom_call" | custom-call | flops 60000002048 | bytes 8000000 | tf_op jit(solution)/shard_map/attention_forward/pallas_call | solution.py:907
  175.9 15.4 %all-to-all-start.1 = ((bf16[16,64,512]{2,1,0:T(8,128)(2,1)}), bf16[16,64,512]{2,1,0:T(8,128)(2,1)S(1)}, u32[]{:S(2)}, u32[]{:S(2)}) async-start(bf16[16,64,512]{2,1,0:T(8,128)(2,1)} %get-tuple-element.36.refs_1_), calls=%async_computation.1 | async-start | bytes 2097152 | tf_op jit(solution)/shard_map/all_to_all | solution.py:1073
  191.3 4.0 pad_maximum_fusion.pieces_ref
  195.3 28.0 %all-to-all-done.1.mixed_ref = bf16[16,64,512]{2,1,0:T(8,128)(2,1)S(1)} async-done(((bf16[16,64,512]{2,1,0:T(8,128)(2,1)}), bf16[16,64,512]{2,1,0:T(8,128)(2,1)S(1)}, u32[]{:S(2)}, u32[]{:S(2)}) %all-to-all-start.1) | async-done | bytes 1048608 | tf_op jit(solution)/shard_map/all_to_all | solution.py:1073
  224.3 98.2 %middle.1 = (bf16[16,64,512]{2,1,0:T(8,128)(2,1)}, f32[1024,1024]{1,0:T(8,128)}, f32[1024,1024]{1,0:T(8,128)}, bf16[1024,1024]{1,0:T(8,128)(2,1)}, bf16[1024,4608]{1,0:T(8,128)(2,1)}, /*index=5*/f32[8,1024]{1,0:T(8,128)}) custom-call(bf16[16,64,512]{2,1,0:T(8,128)(2,1)} %copy-done.4, bf16[1024,1024]{1,0:T(8,128)(2,1)} %tokens_ref.5, ...), custom_call_target="tpu_custom_call" | custom-call | tf_op jit(solution)/shard_map/middle/pallas_call | solution.py:722
  322.5 126.0 %attention_backward.1 = (bf16[16,64,512]{2,1,0:T(8,128)(2,1)}, bf16[2,16,128,512]{3,2,1,0:T(8,128)(2,1)}) custom-call(s32[4]{0:T(128)} %bitcast.36, s32[1]{0:T(128)} %bitcast.2.me_ref, bf16[16,192,512]{2,1,0:T(8,128)(2,1)} %copy-done.1, bf16[2,16,128,512]{3,2,1,0:T(8,128)(2,1)} %pad_maximum_fusion.pieces_ref, ...), custom_call_target="tpu_custom_call" | custom-call | flops 149999992832 | bytes 20000000 | tf_op jit(solution)/shard_map/attention_backward/pallas_call | solution.py:1016
  448.5 1.9 slice_bitcast_fusion
  450.6 4.1 collective-permute-done.2
  454.7 0.7 fusion
  455.4 1.9 pad_maximum_fusion.1
  457.3 3.7 all-to-all-start.2
  461.7 47.4 %collective-permute-done.3 = bf16[1024,1024]{1,0:T(8,128)(2,1)S(1)} collective-permute-done((bf16[1024,1024]{1,0:T(8,128)(2,1)}, bf16[1024,1024]{1,0:T(8,128)(2,1)S(1)}, u32[]{:S(2)}, u32[]{:S(2)}) %collective-permute-start.3) | collective-permute-done | bytes 2097184 | tf_op jit(solution)/shard_map/ppermute | solution.py:1046
  509.1 5.4 add_convert_fusion
  514.5 5.9 all-to-all-done.2.dheads_ref
  520.3 1.7 copy-done
  522.0 67.1 %finish.1 = (f32[1024,1024]{1,0:T(8,128)}, f32[1,64,512]{2,1,0:T(8,128)}, f32[1,64,512]{2,1,0:T(8,128)}, f32[1,64,512]{2,1,0:T(8,128)}, f32[1,2,64]{2,1,0:T(2,128)}, /*index=5*/f32[1,2,64]{2,1,0:T(2,128)}) custom-call(bf16[16,192,512]{2,1,0:T(8,128)(2,1)} %copy-done, bf16[1024,1024]{1,0:T(8,128)(2,1)} %get-tuple-element.47.normed_ref, ...), custom_call_target="tpu_custom_call" | custom-call | tf_op jit(solution)/shard_map/finish/pallas_call | solution.py:407
  589.1 1.1 convert_element_type.31
  590.3 0.7 slice_bitcast_fusion.3
  590.9 1.0 slice_bitcast_fusion.1
  592.0 4.8 copy.27
  596.8 0.7 copy.28
  (41 shorter events, 4.5 us)
Async XLA Ops:
  45.1 4.0 copy-start.11
  45.1 8.7 %copy-start.7 = (bf16[1,2048,64]{1,2,0:T(8,128)(2,1)S(1)}, bf16[1,2048,64]{1,2,0:T(8,128)(2,1)}, u32[]{:S(2)}) copy-start(bf16[1,2048,64]{1,2,0:T(8,128)(2,1)} %param.18) | copy-start | bytes 786436
  45.2 63.2 %all-to-all-start = ((bf16[16,192,512]{2,1,0:T(8,128)(2,1)}), bf16[16,192,512]{2,1,0:T(8,128)(2,1)S(1)}, u32[]{:S(2)}, u32[]{:S(2)}) async-start(bf16[16,192,512]{2,1,0:T(8,128)(2,1)} %get-tuple-element.34), calls=%async_computation | async-start | bytes 6291456 | tf_op jit(solution)/shard_map/all_to_all | solution.py:1073
  49.1 174.7 %all-gather.2.cloned.1.call-start = ((), (), s32[]{:S(2)}) async-start(), calls=%async_computation.4 | async-start | bytes 11141120 | tf_op jit(solution)/shard_map/all_gather | solution.py:1082
  49.1 4.7 collective-permute-start
  108.3 2.9 copy-start.1
  108.4 3.6 copy-start.14
  111.2 4.8 collective-permute-start.1
  116.0 1.4 copy-start.5
  175.9 15.4 %copy-start.2 = (bf16[1,16,128,512]{3,2,1,0:T(8,128)(2,1)S(1)}, bf16[1,16,128,512]{3,2,1,0:T(8,128)(2,1)}, u32[]{:S(2)}) copy-start(bf16[1,16,128,512]{3,2,1,0:T(8,128)(2,1)} %get-tuple-element.58) | copy-start | bytes 6291460
  175.9 47.5 %all-to-all-start.1 = ((bf16[16,64,512]{2,1,0:T(8,128)(2,1)}), bf16[16,64,512]{2,1,0:T(8,128)(2,1)S(1)}, u32[]{:S(2)}, u32[]{:S(2)}) async-start(bf16[16,64,512]{2,1,0:T(8,128)(2,1)} %get-tuple-element.36.refs_1_), calls=%async_computation.1 | async-start | bytes 2097152 | tf_op jit(solution)/shard_map/all_to_all | solution.py:1073
  191.3 397.9 %reduce-scatter.2.cloned.1.call-start = ((), (), s32[]{:S(2)}) async-start(), calls=%async_computation.5 | async-start | bytes 10027008 | tf_op jit(solution)/shard_map/reduce_scatter | solution.py:1094
  223.3 1.0 copy-start.4
  448.5 6.2 %copy-start.3 = (bf16[2,16,128,512]{3,2,1,0:T(8,128)(2,1)S(1)}, bf16[2,16,128,512]{3,2,1,0:T(8,128)(2,1)}, u32[]{:S(2)}) copy-start(bf16[2,16,128,512]{3,2,1,0:T(8,128)(2,1)} %get-tuple-element.44) | copy-start | bytes 12582916
  450.5 4.9 copy-start.6
  450.5 4.2 collective-permute-start.2
  457.3 63.0 %all-to-all-start.2 = ((bf16[16,192,512]{2,1,0:T(8,128)(2,1)}), bf16[16,192,512]{2,1,0:T(8,128)(2,1)S(1)}, u32[]{:S(2)}, u32[]{:S(2)}) async-start(bf16[16,192,512]{2,1,0:T(8,128)(2,1)} %pad_maximum_fusion.1), calls=%async_computation.2 | async-start | bytes 6291456 | tf_op jit(solution)/shard_map/all_to_all | solution.py:1073
  461.0 48.0 %collective-permute-start.3 = (bf16[1024,1024]{1,0:T(8,128)(2,1)}, bf16[1024,1024]{1,0:T(8,128)(2,1)S(1)}, u32[]{:S(2)}, u32[]{:S(2)}) collective-permute-start(bf16[1024,1024]{1,0:T(8,128)(2,1)} %get-tuple-element.45), channel_id=1, source_target_pairs={{0,1},{1,0},{2,3},{3,2},{4,5},{5,4},{6,7},{7,6},{8,9},{9,8},{10,11... | collective-permute-start | bytes 6291464 | tf_op jit(solution)/shard_map/ppermute | solution.py:1046
  520.3 1.7 copy-start
  592.0 4.9 copy-start.10
  592.0 5.5 copy-start.9
  592.0 6.2 %copy-start.8 = (f32[1,64,512]{2,1,0:T(8,128)S(1)}, f32[1,64,512]{2,1,0:T(8,128)}, u32[]{:S(2)}) copy-start(f32[1,64,512]{2,1,0:T(8,128)} %get-tuple-element.76) | copy-start | bytes 393220
  592.0 6.8 %copy-start.13 = (f32[1,2,64]{2,1,0:T(2,128)S(1)}, f32[1,2,64]{2,1,0:T(2,128)}, u32[]{:S(2)}) copy-start(f32[1,2,64]{2,1,0:T(2,128)} %get-tuple-element.80) | copy-start | bytes 1540
  592.0 7.4 %copy-start.12 = (f32[1,2,64]{2,1,0:T(2,128)S(1)}, f32[1,2,64]{2,1,0:T(2,128)}, u32[]{:S(2)}) copy-start(f32[1,2,64]{2,1,0:T(2,128)} %get-tuple-element.81) | copy-start | bytes 1540
Sparse Core Ops, SparseCore 0:
  108.5 115.2 all-gather.1
  322.7 112.3 reduce-scatter.1

commit v2 on v1

--- a/solution.py
+++ b/solution.py
@@ -61,9 +61,9 @@
 
 def project_kernel(
     tokens_ref, query_ref, key_ref, value_ref, gain_ref, bias_ref,
-    sent_ref, normed_ref, weights_ref, norms_ref,
-    gathered, scaled, send_right, recv_right, send_left, recv_left, send_peer, recv_peer,
-    out_sem,
+    recv_ref, others_ref, normed_ref, weights_ref, norms_ref,
+    gathered, scaled, sent, send_right, recv_right, send_left, recv_left, send_peer, recv_peer,
+    head_send, head_recv, home_sem, core_send, core_recv, out_sem,
     *, devices, group, columns, width,
 ):
     chips = devices // 2
@@ -75,7 +75,7 @@
     left = seq_index(lax.rem(place + chips - 1, chips))
     peer = me + 1 - 2 * core
     heads = columns // HEAD_DIM
-    meet([{"seq": right}, {"seq": left}, {"seq": peer}])
+    meet([{"seq": lax.rem(me + step, devices)} for step in range(1, devices)])
 
     def slot(index):
         return gathered.at[pl.ds(pl.multiple_of(index * depth, depth), depth), :]
@@ -160,7 +160,23 @@
         return carry
 
     lax.fori_loop(0, tokens_ref.shape[0] // 128, apply_norm, 0)
-    for which in range(3):
+
+    def head_copy(step, which):
+        where = lax.rem(me + step, devices)
+        at = slice(which * HEAD_DIM, (which + 1) * HEAD_DIM)
+        return remote_copy(
+            sent.at[where, at, :], recv_ref.at[me, at, :], head_send.at[step, which],
+            head_recv.at[me, which], where,
+        )
+
+    def core_copy(source_ref, source):
+        return remote_copy(
+            source_ref.at[source, HEAD_DIM:, :], others_ref.at[0, source], core_send.at[source],
+            core_recv.at[source], peer,
+        )
+
+    home = pltpu.make_async_copy(sent.at[me], recv_ref.at[me], home_sem)
+    for which in (1, 2, 0):
         weights = gathered[:, which * columns : (which + 1) * columns].T
         factor = HEAD_DIM**-0.5 * log2_e if which == 0 else 1.0
 
@@ -168,12 +184,55 @@
             at = pl.ds(pl.multiple_of(core_index * rows, rows), rows)
             result = (dot(weights, normed_ref[at, :], 1, 1) * factor).astype(BF)
             for head in range(heads):
-                sent_ref[head * group + core_index, which * HEAD_DIM : (which + 1) * HEAD_DIM, :] = (
+                sent[head * group + core_index, which * HEAD_DIM : (which + 1) * HEAD_DIM, :] = (
                     result[head * HEAD_DIM : (head + 1) * HEAD_DIM, :]
                 )
             return carry
 
         lax.fori_loop(0, group, project, 0)
+
+        def send(step, carry, which=which):
+            head_copy(step, which).start()
+            return carry
+
+        lax.fori_loop(1, devices, send, 0)
+        if which == 2 and group == 2:
+            core_copy(sent, me).start()
+    home.start()
+
+    def wait_head(step, carry, which):
+        source = lax.rem(me - step + devices, devices)
+        at = slice(which * HEAD_DIM, (which + 1) * HEAD_DIM)
+        remote_copy(
+            sent.at[source, at, :], recv_ref.at[source, at, :], head_send.at[0, which],
+            head_recv.at[source, which], source,
+        ).wait_recv()
+        return carry
+
+    def forward(step, carry):
+        wait_head(step, carry, 1)
+        wait_head(step, carry, 2)
+        if group == 2:
+            core_copy(recv_ref, lax.rem(me - step + devices, devices)).start()
+        return carry
+
+    lax.fori_loop(1, devices, forward, 0)
+    lax.fori_loop(1, devices, functools.partial(wait_head, which=0), 0)
+    home.wait()
+
+    def finish_core(source, carry):
+        core_copy(recv_ref, source).wait()
+        return carry
+
+    if group == 2:
+        lax.fori_loop(0, devices, finish_core, 0)
+
+    def wait_sent(step, carry):
+        for which in range(3):
+            head_copy(step, which).wait_send()
+        return carry
+
+    lax.fori_loop(1, devices, wait_sent, 0)
     for step in range(to_right):
         rightward(step).wait_send()
     for step in range(to_left):
@@ -187,16 +246,19 @@
     own_rows, width = tokens.shape
     columns = w_query.shape[2]
     chips = devices // 2
+    rows = own_rows // group
     whole = pl.BlockSpec(memory_space=pltpu.VMEM)
+    far = pl.BlockSpec(memory_space=pl.ANY)
     dma = pltpu.SemaphoreType.DMA
     return pl.pallas_call(
         functools.partial(
             project_kernel, devices=devices, group=group, columns=columns, width=width
         ),
         in_specs=[whole] * 6,
-        out_specs=[whole, whole, pl.BlockSpec(memory_space=pl.ANY), whole],
+        out_specs=[far, far, whole, far, whole],
         out_shape=[
-            jax.ShapeDtypeStruct((devices, 3 * HEAD_DIM, own_rows // group), BF),
+            jax.ShapeDtypeStruct((devices, 3 * HEAD_DIM, rows), BF),
+            jax.ShapeDtypeStruct((1, devices, 2 * HEAD_DIM, rows), BF),
             jax.ShapeDtypeStruct((own_rows, width), BF),
             jax.ShapeDtypeStruct((width, 3 * columns), BF),
             jax.ShapeDtypeStruct((8, width), F32),
@@ -204,9 +266,12 @@
         scratch_shapes=[
             pltpu.VMEM((width, 3 * columns + 128), BF),
             pltpu.VMEM((own_rows, width), F32),
+            pltpu.VMEM((devices, 3 * HEAD_DIM, rows), BF),
             dma((chips // 2,)), dma((chips // 2,)),
             dma((chips // 2,)), dma((chips // 2,)),
             dma((chips,)), dma((chips,)),
+            dma((devices, 3)), dma((devices, 3)), dma,
+            dma((devices,)), dma((devices,)),
             dma,
         ],
         compiler_params=pltpu.CompilerParams(
@@ -217,28 +282,50 @@
 
 
 def finish_kernel(
-    dheads_ref, normed_ref, weights_ref, tokens_ref, dmid_ref, norms_ref, second_ref,
-    dstream_ref, dquery_ref, dkey_ref, dvalue_ref, dgain_ref, dbias_ref,
-    flat, partial_sent, partial_got, partial, from_peer, first_right, first_left,
-    ring_right, ring_left, total, few_sent, few_got,
-    x_send, x_recv, peer_send, peer_recv, right_send, right_recv, left_send, left_recv,
-    few_send, few_recv,
-    *, devices, group, columns, width,
+    dquery_ref, dpieces_far, normed_far, weights_far, tokens_far, dmid_far, mid_far, z_far,
+    z_other_far, norms_ref, second_ref,
+    dstream_far, last_far, dquery_w_ref, dkey_w_ref, dvalue_w_ref, dgain_ref, dbias_ref,
+    normed, weights, tokens, dmid, mid, z, z_other, own_piece,
+    core_got, sent, got, flat, partial_sent, partial_got, summed_grads, partial, from_peer,
+    first_right, first_left, ring_right, ring_left, total, few_sent, few_got,
+    load_sem, store_sem, core_send, core_recv, head_send, head_recv, x_send, x_recv,
+    peer_send, peer_recv, right_send, right_recv, left_send, left_recv, few_send, few_recv,
+    *, devices, group, cores, columns, width,
 ):
     chips = devices // 2
     depth = width // devices
-    own_rows = tokens_ref.shape[0]
+    own_rows = tokens.shape[0]
     rows = own_rows // group
     heads = columns // HEAD_DIM
     wide = 3 * columns + 128
     cut = first_right.shape[1]
+    lanes = 128
+    chunks = rows // lanes
     place, core, seq_index = ring_of(devices)
     me = seq_index(place)
     right = {"seq": seq_index(lax.rem(place + 1, chips))}
     left = {"seq": seq_index(lax.rem(place + chips - 1, chips))}
     peer = {"seq": me + 1 - 2 * core}
     across = {"tensor": 1 - lax.axis_index("tensor")}
-    meet([right, left, peer, across])
+    group_place = lax.rem(me, group)
+
+    loads = {}
+    for number, (name, far, near) in enumerate((
+        ("piece", dpieces_far.at[0], own_piece), ("tokens", tokens_far, tokens), ("weights", weights_far, weights),
+        ("normed", normed_far, normed), ("z", z_far, z), ("z_other", z_other_far, z_other),
+        ("mid", mid_far, mid), ("dmid", dmid_far, dmid),
+    )):
+        loads[name] = pltpu.make_async_copy(far, near, load_sem.at[number])
+        loads[name].start()
+
+    barrier = pltpu.get_barrier_semaphore()
+    for step in range(1, devices):
+        pl.semaphore_signal(
+            barrier, inc=1, device_id={"seq": lax.rem(me + step, devices)},
+            device_id_type=pl.DeviceIdType.MESH,
+        )
+    pl.semaphore_signal(barrier, inc=1, device_id=across, device_id_type=pl.DeviceIdType.MESH)
+    pl.semaphore_wait(barrier, devices)
 
     def copy_to(source, target, send_sem, recv_sem, where):
         return pltpu.make_async_remote_copy(
@@ -246,50 +333,164 @@
             device_id=where, device_id_type=pl.DeviceIdType.MESH,
         )
 
-    def flatten(index, carry):
-        head = index // group
-        part = lax.rem(index, group)
-        at = pl.ds(pl.multiple_of(part * rows, rows), rows)
-        for which in range(3):
-            to = pl.ds(
-                pl.multiple_of(which * columns + head * HEAD_DIM, HEAD_DIM), HEAD_DIM
-            )
-            flat[to, at] = dheads_ref[index, which * HEAD_DIM : (which + 1) * HEAD_DIM, :]
+    def core_copy(by, chunk):
+        other = jnp.int32(0)
+        bit = 1
+        while bit < group:
+            mine = lax.rem(group_place // bit, 2)
+            other = other + bit * ((1 - mine) if by & bit else mine)
+            bit *= 2
+        at = slice(chunk * lanes, (chunk + 1) * lanes)
+        return copy_to(
+            dpieces_far.at[by, :, :, at], core_got.at[by - 1, :, :, at],
+            core_send.at[by - 1, chunk], core_recv.at[by - 1, chunk],
+            {"seq": me - group_place + other},
+        )
+
+    def head_copy(step, chunk):
+        where = lax.rem(me + step, devices)
+        at = slice(chunk * lanes, (chunk + 1) * lanes)
+        return copy_to(
+            sent.at[where, :, at], got.at[me, :, at],
+            head_send.at[step, chunk], head_recv.at[me, chunk], {"seq": where},
+        )
+
+    for chunk in range(chunks):
+        for by in range(1, cores):
+            core_copy(by, chunk).start()
+    loads["piece"].wait()
+    for chunk in range(chunks):
+        at = slice(chunk * lanes, (chunk + 1) * lanes)
+        for by in range(1, cores):
+            core_copy(by, chunk).wait_recv()
+
+        def gather(index, carry, at=at):
+            piece = own_piece[index, :, at].astype(F32)
+            for by in range(1, cores):
+                piece = piece + core_got[by - 1, index, :, at].astype(F32)
+            sent[index, HEAD_DIM:, at] = piece.astype(BF)
+            sent[index, 0:HEAD_DIM, at] = dquery_ref[index, :, at]
+            return carry
+
+        lax.fori_loop(0, devices, gather, 0)
+
+        def send(step, carry, chunk=chunk):
+            head_copy(step, chunk).start()
+            return carry
+
+        lax.fori_loop(1, devices, send, 0)
+
+    loads["z"].wait()
+    loads["z_other"].wait()
+    loads["mid"].wait()
+
+    def add_last(index, carry):
+        at = pl.ds(pl.multiple_of(index * lanes, lanes), lanes)
+        both = z[at, :].astype(F32) + z_other[at, :].astype(F32)
+        z[at, :] = (mid[at, :] + both).astype(BF)
         return carry
 
-    lax.fori_loop(0, devices, flatten, 0)
-
-    parts = 4
-    part_rows = own_rows // parts
-
-    def x_copy(part):
-        at = pl.ds(part * part_rows, part_rows)
+    lax.fori_loop(0, own_rows // lanes, add_last, 0)
+    store_last = pltpu.make_async_copy(z, last_far, store_sem.at[0])
+    store_last.start()
+    for name in ("tokens", "weights", "normed", "dmid"):
+        loads[name].wait()
+
+    def part_rows(place_in_group, chunk):
+        return slice(place_in_group * rows + chunk * lanes, place_in_group * rows + (chunk + 1) * lanes)
+
+    def x_copy(place_in_group, chunk):
+        at = part_rows(place_in_group, chunk)
+        number = place_in_group * chunks + chunk
         return copy_to(
-            partial_sent.at[at, :], partial_got.at[at, :], x_send.at[part], x_recv.at[part], across
+            partial_sent.at[at, :], partial_got.at[at, :], x_send.at[number], x_recv.at[number],
+            across,
         )
 
     def unit_rows(at):
-        stream = tokens_ref[at, :].astype(F32)
+        stream = tokens[at, :].astype(F32)
         centred = stream - jnp.mean(stream, axis=-1, keepdims=True)
         spread = jnp.mean(centred * centred, axis=-1, keepdims=True)
         inverse = lax.rsqrt(spread + norm_eps)
         return centred * inverse, inverse
 
+    def finish_norm(chunk):
+        for place_in_group in range(group):
+            at = part_rows(place_in_group, chunk)
+            x_copy(place_in_group, chunk).wait_recv()
+            dnormed = partial_sent[at, :].astype(F32) + partial_got[at, :].astype(F32)
+            unit, inverse = unit_rows(at)
+            dunit = dnormed * norms_ref[0:1, :]
+            mean = jnp.mean(dunit, axis=-1, keepdims=True)
+            along = jnp.mean(dunit * unit, axis=-1, keepdims=True)
+            dmid[at, :] = dmid[at, :] + (dunit - mean - unit * along) * inverse
+
     gain_sum = jnp.zeros((1, width), F32)
     bias_sum = jnp.zeros((1, width), F32)
-    for part in range(parts):
-        at = pl.ds(part * part_rows, part_rows)
-        result = dot(flat[:, at].T, weights_ref[...], 1, 1)
-        partial_sent[at, :] = result.astype(BF)
-        x_copy(part).start()
-        unit, _ = unit_rows(at)
-        gain_sum = gain_sum + jnp.sum(result * unit, axis=0, keepdims=True)
-        bias_sum = bias_sum + jnp.sum(result, axis=0, keepdims=True)
-
     lines = 256
-    for line in range(width // lines):
-        at = slice(line * lines, (line + 1) * lines)
-        partial[at, 0 : 3 * columns] = dot(normed_ref[:, at].T, flat[...], 1, 1).astype(BF)
+    for chunk in range(chunks):
+        at = slice(chunk * lanes, (chunk + 1) * lanes)
+
+        def flatten(index, carry, chunk=chunk, at=at):
+            head = index // group
+            start = lax.rem(index, group) * rows + chunk * lanes
+            to_rows = pl.ds(pl.multiple_of(start, lanes), lanes)
+
+            def put(source):
+                for which in range(3):
+                    to = pl.ds(
+                        pl.multiple_of(which * columns + head * HEAD_DIM, HEAD_DIM), HEAD_DIM
+                    )
+                    flat[to, to_rows] = source[index, which * HEAD_DIM : (which + 1) * HEAD_DIM, at]
+
+            @pl.when(index == me)
+            def _():
+                put(sent)
+
+            @pl.when(index != me)
+            def _():
+                copy_to(
+                    sent.at[index, :, at], got.at[index, :, at],
+                    head_send.at[0, chunk], head_recv.at[index, chunk], {"seq": index},
+                ).wait_recv()
+                put(got)
+
+            return carry
+
+        lax.fori_loop(0, devices, flatten, 0)
+        ats = [part_rows(place_in_group, chunk) for place_in_group in range(group)]
+        flat_chunk = jnp.concatenate([flat[:, part] for part in ats], axis=1)
+
+        def sum_grads():
+            normed_t = jnp.concatenate([normed[part, :] for part in ats], axis=0).T
+            for line in range(width // lines):
+                here = slice(line * lines, (line + 1) * lines)
+                result = dot(normed_t[here, :], flat_chunk, 1, 1)
+                if chunk > 0:
+                    result = result + summed_grads[here, :]
+                if chunk + 1 < chunks:
+                    summed_grads[here, :] = result
+                else:
+                    partial[here, 0 : 3 * columns] = result.astype(BF)
+
+        def send_dnormed(gain_sum, bias_sum):
+            result = dot(flat_chunk.T, weights[...], 1, 1)
+            for place_in_group in range(group):
+                here = slice(place_in_group * lanes, (place_in_group + 1) * lanes)
+                partial_sent[ats[place_in_group], :] = result[here, :].astype(BF)
+                x_copy(place_in_group, chunk).start()
+            for place_in_group in range(group):
+                here = slice(place_in_group * lanes, (place_in_group + 1) * lanes)
+                unit, _ = unit_rows(ats[place_in_group])
+                gain_sum = gain_sum + jnp.sum(result[here, :] * unit, axis=0, keepdims=True)
+                bias_sum = bias_sum + jnp.sum(result[here, :], axis=0, keepdims=True)
+            return gain_sum, bias_sum
+
+        gain_sum, bias_sum = send_dnormed(gain_sum, bias_sum)
+        sum_grads()
+        if chunk > 0 and chunk + 1 < chunks:
+            finish_norm(chunk - 1)
+
     norm_rows = jnp.concatenate(
         [
             gain_sum, second_ref[0:1, :] * 0.5, bias_sum, second_ref[1:2, :] * 0.5,
@@ -327,23 +528,8 @@
             waited.append(number)
         where = lax.rem(place + offset % chips, chips)
         own = pl.ds(pl.multiple_of(seq_index(where) * depth, depth), depth)
-        got = pl.ds(pl.multiple_of(where * depth, depth), depth)
-        return partial[own, low:high].astype(F32) + from_peer[got, low:high].astype(F32)
-
-    def finish_norm(part):
-        x_copy(part).wait_recv()
-
-        def piece(index, carry):
-            at = pl.ds(pl.multiple_of(part * part_rows + index * 128, 128), 128)
-            dnormed = partial_sent[at, :].astype(F32) + partial_got[at, :].astype(F32)
-            unit, inverse = unit_rows(at)
-            dunit = dnormed * norms_ref[0:1, :]
-            mean = jnp.mean(dunit, axis=-1, keepdims=True)
-            along = jnp.mean(dunit * unit, axis=-1, keepdims=True)
-            dstream_ref[at, :] = dmid_ref[at, :] + (dunit - mean - unit * along) * inverse
-            return carry
-
-        lax.fori_loop(0, part_rows // 128, piece, 0)
+        there = pl.ds(pl.multiple_of(where * depth, depth), depth)
+        return partial[own, low:high].astype(F32) + from_peer[there, low:high].astype(F32)
 
     steps = chips - 1
 
@@ -360,9 +546,10 @@
     ring_copy(0, True).start()
     first_left[...] = chip_block(1, cut, wide).astype(BF)
     ring_copy(0, False).start()
+    pending = list(range(max(chunks - 2, 0), chunks))
     for step in range(steps):
-        if step in (0, steps // 2, steps - 1):
-            finish_norm((0, steps // 2, steps - 1).index(step))
+        if pending and step in (1, steps // 2):
+            finish_norm(pending.pop(0))
         for toward_right, ring, low, high in (
             (True, ring_right, 0, cut), (False, ring_left, cut, wide),
         ):
@@ -377,66 +564,93 @@
     few_sent[...] = total[:, 3 * columns :]
     few = copy_to(few_sent, few_got, few_send, few_recv, across)
     few.start()
-    dquery_ref[0] = total[:, 0:columns]
-    dkey_ref[0] = total[:, columns : 2 * columns]
-    dvalue_ref[0] = total[:, 2 * columns : 3 * columns]
-    finish_norm(3)
+    for chunk in pending:
+        finish_norm(chunk)
+    store_stream = pltpu.make_async_copy(dmid, dstream_far, store_sem.at[1])
+    store_stream.start()
+    dquery_w_ref[0] = total[:, 0:columns]
+    dkey_w_ref[0] = total[:, columns : 2 * columns]
+    dvalue_w_ref[0] = total[:, 2 * columns : 3 * columns]
     few.wait()
     norm_rows = (few_sent[...] + few_got[...]).T
     dgain_ref[0] = norm_rows[0:2, :]
     dbias_ref[0] = norm_rows[2:4, :]
-    for part in range(parts):
-        x_copy(part).wait_send()
+    for chunk in range(chunks):
+        for by in range(1, cores):
+            core_copy(by, chunk).wait_send()
+        for place_in_group in range(group):
+            x_copy(place_in_group, chunk).wait_send()
+
+        def wait_head(step, carry, chunk=chunk):
+            head_copy(step, chunk).wait_send()
+            return carry
+
+        lax.fori_loop(1, devices, wait_head, 0)
     for number in range(chips):
         peer_copy(number).wait_send()
     for step in range(steps):
         ring_copy(step, True).wait_send()
         ring_copy(step, False).wait_send()
-
-
-def finish(dheads, normed, weights, tokens, dmid, norms, second, devices, group):
+    store_last.wait()
+    store_stream.wait()
+
+
+def finish(
+    dquery, dpieces, normed, weights, tokens, dmid, mid, z, z_other, norms, second, devices, group
+):
     own_rows, width = tokens.shape
+    cores, _, _, rows = dpieces.shape
     columns = weights.shape[1] // 3
     chips = devices // 2
     depth = width // devices
     wide = 3 * columns + 128
     cut = (wide // 128 + 1) // 2 * 128
     steps = chips - 1
+    chunks = rows // 128
     whole = pl.BlockSpec(memory_space=pltpu.VMEM)
+    far = pl.BlockSpec(memory_space=pl.ANY)
     dma = pltpu.SemaphoreType.DMA
+    vmem = pltpu.VMEM
     return pl.pallas_call(
         functools.partial(
-            finish_kernel, devices=devices, group=group, columns=columns, width=width
+            finish_kernel, devices=devices, group=group, cores=cores, columns=columns, width=width
         ),
-        in_specs=[whole] * 7,
-        out_specs=[whole] * 6,
-        out_shape=[jax.ShapeDtypeStruct((own_rows, width), F32)]
+        in_specs=[whole] + [far] * 8 + [whole] * 2,
+        out_specs=[far] * 2 + [whole] * 5,
+        out_shape=[
+            jax.ShapeDtypeStruct((own_rows, width), F32),
+            jax.ShapeDtypeStruct((own_rows, width), BF),
+        ]
         + [jax.ShapeDtypeStruct((1, depth, columns), F32)] * 3
         + [jax.ShapeDtypeStruct((1, 2, depth), F32)] * 2,
         scratch_shapes=[
-            pltpu.VMEM((3 * columns, own_rows), BF),
-            pltpu.VMEM((own_rows, width), BF),
-            pltpu.VMEM((own_rows, width), BF),
-            pltpu.VMEM((width, wide), BF),
-            pltpu.VMEM((chips * depth, wide), BF),
-            pltpu.VMEM((depth, cut), BF),
-            pltpu.VMEM((depth, wide - cut), BF),
-            pltpu.VMEM((steps, depth, cut), BF),
-            pltpu.VMEM((steps, depth, wide - cut), BF),
-            pltpu.VMEM((depth, wide), F32),
-            pltpu.VMEM((depth, 128), F32),
-            pltpu.VMEM((depth, 128), F32),
-            dma((4,)), dma((4,)),
+            vmem((own_rows, width), BF), vmem((width, 3 * columns), BF),
+            vmem((own_rows, width), BF), vmem((own_rows, width), F32),
+            vmem((own_rows, width), F32), vmem((own_rows, width), BF),
+            vmem((own_rows, width), BF), vmem((devices, 128, rows), BF),
+            vmem((max(cores - 1, 1), devices, 128, rows), BF),
+            vmem((devices, 3 * HEAD_DIM, rows), BF), vmem((devices, 3 * HEAD_DIM, rows), BF),
+            vmem((3 * columns, own_rows), BF),
+            vmem((own_rows, width), BF), vmem((own_rows, width), BF),
+            vmem((width, 3 * columns), F32), vmem((width, wide), BF),
+            vmem((chips * depth, wide), BF),
+            vmem((depth, cut), BF), vmem((depth, wide - cut), BF),
+            vmem((steps, depth, cut), BF), vmem((steps, depth, wide - cut), BF),
+            vmem((depth, wide), F32),
+            vmem((depth, 128), F32), vmem((depth, 128), F32),
+            dma((8,)), dma((2,)),
+            dma((max(cores - 1, 1), chunks)), dma((max(cores - 1, 1), chunks)),
+            dma((devices, chunks)), dma((devices, chunks)),
+            dma((group * chunks,)), dma((group * chunks,)),
             dma((chips,)), dma((chips,)),
-            dma((steps,)), dma((steps,)),
-            dma((steps,)), dma((steps,)),
+            dma((steps,)), dma((steps,)), dma((steps,)), dma((steps,)),
             dma, dma,
         ],
         compiler_params=pltpu.CompilerParams(
-            vmem_limit_bytes=VMEM_BYTES, collective_id=2, has_side_effects=True
+            vmem_limit_bytes=60 * 2**20, collective_id=2, has_side_effects=True
         ),
         name="finish",
-    )(dheads, normed, weights, tokens, dmid, norms, second)
+    )(dquery, dpieces, normed, weights, tokens, dmid, mid, z, z_other, norms, second)
 
 
 def middle_kernel(
@@ -934,7 +1148,7 @@
     )(ends, me, recv, other)
 
 
-def backward_kernel(ends_ref, me_ref, recv_ref, pieces_ref, *refs, scenes, group, parts):
+def backward_kernel(ends_ref, me_ref, recv_ref, others_ref, *refs, scenes, group, parts):
     dout_refs = refs[:parts]
     out_ref, lse_ref, dquery_ref, dkeys_ref = refs[parts : parts + 4]
     queries, douts, queries_flat, douts_flat, dqueries = refs[parts + 4 :]
@@ -972,12 +1186,20 @@
     first = block * rows
     low, high = scene_span(ends_ref, scenes, first, first + rows - 1)
     extra = key_extra(ends_ref, scenes, first, rows)
-    key = pieces_ref[0, 0, 0:64, :]
+    own = place == core
+    key = jnp.where(own, recv_ref[source, 64:128, :], others_ref[0, 0, 0:64, :])
+    value = jnp.where(own, recv_ref[source, 128:192, :], others_ref[0, 0, 64:128, :])
     key_wide = jnp.concatenate([key, extra], axis=0)
-    value_wide = jnp.concatenate([pieces_ref[0, 0, 64:128, :], extra], axis=0)
-    key_rows = key.T
-    begin = (low - core * rows - rows + span) // span
-    count = jnp.minimum((high - core * rows + span - 1) // span, sources) - begin
+    value_wide = jnp.concatenate([value, extra], axis=0)
+    key_rows = key_wide.T
+    unit = min(256, rows)
+
+    def local(position):
+        inside = jnp.clip(lax.rem(position, span) - core * rows, 0, rows)
+        return position // span * rows + inside
+
+    begin = local(low) // unit
+    count = (local(high) + unit - 1) // unit - begin
 
     def process(offset, size, carry):
         dkey, dvalue = carry
@@ -991,7 +1213,7 @@
         return dkey, dvalue
 
     zeros = jnp.zeros((64, rows), F32)
-    dkey, dvalue = walk_tiles(process, (zeros, zeros), begin, count, rows, (4, 2, 1))
+    dkey, dvalue = walk_tiles(process, (zeros, zeros), begin, count, unit, (8, 4, 2, 1))
     dkeys_ref[0, 0, 0:64, :] = (dkey * ln_2).astype(BF)
     dkeys_ref[0, 0, 64:128, :] = dvalue.astype(BF)
 
@@ -999,16 +1221,19 @@
     def _():
         def store(source, carry):
             at = pl.ds(pl.multiple_of(source * rows, rows), rows)
-            dquery_ref[source] = (dqueries[at, :].T * HEAD_DIM**-0.5).astype(BF)
+            dquery_ref[source] = (dqueries[at, :].T[0:64, :] * HEAD_DIM**-0.5).astype(BF)
             return carry
 
         lax.fori_loop(0, sources, store, 0)
 
 
-def attention_backward(ends, me, recv, pieces, dout, out, lse, group):
+def attention_backward(ends, me, recv, others, dout, out, lse, group):
     sources, _, rows = recv.shape
     mine = sources * rows
     whole = pl.BlockSpec(memory_space=pltpu.VMEM)
+
+    def other_map(block, ends_ref, me_ref):
+        return (jnp.maximum((block % group) ^ me_ref[0], 1) - 1, block // group, 0, 0)
 
     def piece_map(block, ends_ref, me_ref):
         return ((block % group) ^ me_ref[0], block // group, 0, 0)
@@ -1020,14 +1245,14 @@
         grid_spec=pltpu.PrefetchScalarGridSpec(
             num_scalar_prefetch=2,
             grid=(sources * group,),
-            in_specs=[whole, pl.BlockSpec((1, 1, 128, rows), piece_map)] + [whole] * (len(dout) + 2),
+            in_specs=[whole, pl.BlockSpec((1, 1, 128, rows), other_map)] + [whole] * (len(dout) + 2),
             out_specs=[whole, pl.BlockSpec((1, 1, 128, rows), piece_map)],
             scratch_shapes=[
                 pltpu.VMEM((mine, 128), BF),
                 pltpu.VMEM((mine, 128), BF),
                 pltpu.VMEM((64, mine), BF),
                 pltpu.VMEM((64, mine), BF),
-                pltpu.VMEM((mine, 64), F32),
+                pltpu.VMEM((mine, 128), F32),
             ],
         ),
         out_shape=[
@@ -1039,7 +1264,7 @@
             flops=150 * 10**9, bytes_accessed=20 * 10**6, transcendentals=45 * 10**6
         ),
         name="attention_backward",
-    )(ends, me, recv, pieces, *dout, out, lse)
+    )(ends, me, recv, others, *dout, out, lse)
 
 
 def swap_tensor(part):
@@ -1072,42 +1297,38 @@
     def to_owners(parts):
         return lax.all_to_all(parts, "seq", 0, 0, tiled=True)
 
-    projected, normed_one, w_first, norms = project(
+    recv, others, normed_one, w_first, norms = project(
         tokens, w_query, w_key, w_value, norm_gain, norm_bias, devices, group
     )
     out_part = in_order(w_out[0].T)
     second_part = jnp.concatenate([out_part, w_up[0], w_down[0].T], axis=1)
-    recv = to_owners(projected)
     recv, second_part = lax.optimization_barrier((recv, second_part))
     second_all = lax.all_gather(second_part, "seq", axis=0, tiled=True)
-    own_piece = recv[:, HEAD_DIM:, :]
-
     def swap_core(part, by):
         return lax.ppermute(part, "seq", [(i, i ^ by) for i in range(devices)])
 
-    others = jnp.stack([swap_core(own_piece, by) for by in range(1, group)])
+    if group > 2:
+        others = jnp.stack([swap_core(recv[:, HEAD_DIM:, :], by) for by in range(1, group)])
     out_head, lse = attention_forward(ends, me, recv, others, group)
 
     dout, dmid, mid, z, grads_second, second_norms = middle(
         to_owners(out_head), tokens, cotangent, second_all, norms, devices, group, columns
     )
+    z_other = swap_tensor(z)
     grads_second = lax.psum_scatter(grads_second, "seq", scatter_dimension=0, tiled=True)
     grads_second = grads_second.astype(F32)
 
-    pieces = jnp.concatenate([own_piece[None], others], axis=0)
-    dquery, dpieces = attention_backward(ends, me, recv, pieces, [dout], out_head, lse, group)
-    dpiece = dpieces[0].astype(F32)
-    for by in range(1, group):
-        dpiece = dpiece + swap_core(dpieces[by], by).astype(F32)
-    dsent = jnp.concatenate([dquery, dpiece.astype(BF)], axis=1)
-    z, dsent = lax.optimization_barrier((z, dsent))
-    dheads = to_owners(dsent)
-    last = mid + (z.astype(F32) + swap_tensor(z).astype(F32))
-    dstream, dquery_w, dkey_w, dvalue_w, dgain, dbias = finish(
-        dheads, normed_one, w_first, tokens, dmid, norms, second_norms, devices, group
+    dquery, dpieces = attention_backward(ends, me, recv, others, [dout], out_head, lse, group)
+    if group > 2:
+        dpieces = sum([dpieces[0].astype(F32)] + [
+            swap_core(dpieces[by], by).astype(F32) for by in range(1, group)
+        ]).astype(BF)[None]
+    dstream, last, dquery_w, dkey_w, dvalue_w, dgain, dbias = finish(
+        dquery, dpieces, normed_one, w_first, tokens, dmid, mid, z, z_other, norms, second_norms,
+        devices, group,
     )
     return (
-        last.astype(BF),
+        last,
         dstream,
         dquery_w,
         dkey_w,

time: 609 us -> 577 us (0.947); the launches traced: 607 us -> 566 us
  waiting for transfers between devices: 145 us -> 2.13 us
  Pallas kernels: 388 us -> 481 us
  blocking collectives: 0 us -> 52.8 us
  starting transfers between devices: 26.1 us -> 3.34 us
  other arithmetic: 15.7 us -> 2.88 us
  local copies, waits for them, and re-layouts: 18.1 us -> 9.79 us
    all_to_all x3 -> x0, waiting for transfers between devices: 86.5 us -> none  [to_owners(): return lax.all_to_all(parts, 'seq', 0, 0, tiled=True)]
    pallas_call x1, Pallas kernels: 37.9 us -> 96.3 us  [project(): pl.pallas_call(functools.partial(project_kernel, devices=devices, group=g...]
    all_to_all x0 -> x1, blocking collectives: none -> 52.8 us  [to_owners(): return lax.all_to_all(parts, 'seq', 0, 0, tiled=True)]
    ppermute x2, waiting for transfers between devices: 50.6 us -> 0.01 us  [swap_tensor(): return lax.ppermute(part, 'tensor', [(0, 1), (1, 0)])]
    pallas_call x1, Pallas kernels: 67.1 us -> 116 us  [finish(): pl.pallas_call(functools.partial(finish_kernel, devices=devices, group=gr...]
    all_to_all x3 -> x0, starting transfers between devices: 23 us -> none  [to_owners(): return lax.all_to_all(parts, 'seq', 0, 0, tiled=True)]
    pallas_call x1, Pallas kernels: 98.2 us -> 81.2 us  [middle(): pl.pallas_call(functools.partial(middle_kernel, devices=devices, group=gr...]
    ppermute x2 -> x0, waiting for transfers between devices: 7.46 us -> none  [swap_core(): return lax.ppermute(part, 'seq', [(i, i ^ by) for i in range(devices)])]
  transfers between devices with their start and end apart: 9 -> 4, of which waited for: 8 -> 1; matrix products, arithmetic and copies ran while one was open for 3% -> 0% of each run, Pallas kernels for 41% -> 71%
where the time goes in v2:
time: 577 us; the launch traced here: 566 us
  Pallas kernels  481 us (83%)
  blocking collectives  52.8 us (9%)
  between operations  14.6 us (3%)
  local copies, waits for them, and re-layouts  9.79 us (2%)
    pallas_call x1, Pallas kernels, attention_backward(): pl.pallas_call(functools.partial(backward_kernel, scenes=ends.shape[0], g...  130 us
    pallas_call x1, Pallas kernels, finish(): pl.pallas_call(functools.partial(finish_kernel, devices=devices, group=gr...  116 us
    pallas_call x1, Pallas kernels, project(): pl.pallas_call(functools.partial(project_kernel, devices=devices, group=g...  96.3 us
    pallas_call x1, Pallas kernels, middle(): pl.pallas_call(functools.partial(middle_kernel, devices=devices, group=gr...  81.2 us
    pallas_call x1, Pallas kernels, attention_forward(): pl.pallas_call(functools.partial(forward_kernel, scenes=ends.shape[0], gr...  56.7 us
    all_to_all x1, blocking collectives, to_owners(): return lax.all_to_all(parts, 'seq', 0, 0, tiled=True)  52.8 us
  transfers between devices with their start and end apart: 4, of which 1 were waited for; matrix products, arithmetic and copies ran while one was open for 0% of the time, Pallas kernels for 71%

profile of v2, /device:TPU:0, one launch (start us, length us, event | category | flops | bytes accessed | tf_op | source)
XLA Modules:
  0.0 566.1 jit_solution(13135786723065047540)
XLA Ops:
  7.2 0.0 copy-start.7
  7.2 0.0 all-gather.2.cloned.1.call-start
  7.3 3.0 collective-permute-start
  10.3 96.3 %project.1 = (bf16[16,192,512]{2,1,0:T(8,128)(2,1)}, bf16[1,16,128,512]{3,2,1,0:T(8,128)(2,1)}, bf16[1024,1024]{1,0:T(8,128)(2,1)}, bf16[1024,1536]{1,0:T(8,128)(2,1)}, f32[8,1024]{1,0:T(8,128)}) custom-call(bf16[1024,1024]{1,0:T(8,128)(2,1)} %tokens_far.1, bf16[1,64,512]{2,1,0:T(8,128)(2,1)} %query_ref.1, bf16[1,64,512]{2,1,0:T(8,128)(2,1)} %key_ref.1, ...), custom_call_target="tpu_custom_call" | custom-call | tf_op jit(solution)/shard_map/project/pallas_call | solution.py:253
  106.6 0.0 collective-permute-done
  106.7 0.9 pad_maximum_fusion
  107.5 0.0 all-gather.2.cloned.1.call-update
  107.6 0.0 reduce-scatter.2.cloned.1.call-start
  107.6 0.7 reduce-window.9
  108.3 56.7 %attention_forward.1 = (bf16[16,64,512]{2,1,0:T(8,128)(2,1)}, f32[16,1,512]{2,1,0:T(1,128)}) custom-call(s32[4]{0:T(128)} %bitcast.25, s32[1]{0:T(128)} %bitcast.2.me_ref, bf16[16,192,512]{2,1,0:T(8,128)(2,1)} %get-tuple-element.35.recv_ref, bf16[1,16,128,512]{3,2,1,0:T(8,128)(2,1)} %get-tuple-element.36.other_ref.others_ref), custom_call_target="tpu_custom_call" | custom-call | flops 60000002048 | bytes 8000000 | tf_op jit(solution)/shard_map/attention_forward/pallas_call | solution.py:1121
  165.0 52.8 %all_to_all.5.mixed_ref = bf16[16,64,512]{2,1,0:T(8,128)(2,1)} all-to-all(bf16[16,64,512]{2,1,0:T(8,128)(2,1)} %get-tuple-element.37.refs_1_), channel_id=1, replica_groups=mesh['seq'=16,'tensor'=2] {'seq'}, dimensions={0} | all-to-all | bytes 2097152 | tf_op jit(solution)/shard_map/all_to_all | solution.py:1298
  217.8 2.1 all-gather.2.cloned.1.call-done.second_ref
  219.8 81.2 %middle.1 = (bf16[16,64,512]{2,1,0:T(8,128)(2,1)}, f32[1024,1024]{1,0:T(8,128)}, f32[1024,1024]{1,0:T(8,128)}, bf16[1024,1024]{1,0:T(8,128)(2,1)}, bf16[1024,4608]{1,0:T(8,128)(2,1)}, /*index=5*/f32[8,1024]{1,0:T(8,128)}) custom-call(bf16[16,64,512]{2,1,0:T(8,128)(2,1)} %all_to_all.5.mixed_ref, bf16[1024,1024]{1,0:T(8,128)(2,1)} %tokens_far.1, ...), custom_call_target="tpu_custom_call" | custom-call | tf_op jit(solution)/shard_map/middle/pallas_call | solution.py:936
  301.0 0.0 reduce-scatter.2.cloned.1.call-update
  301.1 0.3 collective-permute-start.1
  301.3 130.2 %attention_backward.1 = (bf16[16,64,512]{2,1,0:T(8,128)(2,1)}, bf16[2,16,128,512]{3,2,1,0:T(8,128)(2,1)}) custom-call(s32[4]{0:T(128)} %bitcast.26, s32[1]{0:T(128)} %bitcast.2.me_ref, bf16[16,192,512]{2,1,0:T(8,128)(2,1)} %get-tuple-element.35.recv_ref, bf16[1,16,128,512]{3,2,1,0:T(8,128)(2,1)} %get-tuple-element.36.other_ref.others_ref, ...), custom_call_target="tpu_custom_call" | custom-call | flops 149999992832 | bytes 20000000 | tf_op jit(solution)/shard_map/attention_backward/pallas_call | solution.py:1241
  431.6 0.0 collective-permute-done.1.z_other_far
  431.6 116.1 %finish.1 = (f32[1024,1024]{1,0:T(8,128)}, bf16[1024,1024]{1,0:T(8,128)(2,1)}, f32[1,64,512]{2,1,0:T(8,128)}, f32[1,64,512]{2,1,0:T(8,128)}, f32[1,64,512]{2,1,0...) custom-call(bf16[16,64,512]{2,1,0:T(8,128)(2,1)} %get-tuple-element.42.dquery_ref, ...), custom_call_target="tpu_custom_call" | custom-call | tf_op jit(solution)/shard_map/finish/pallas_call | solution.py:614
  547.7 0.0 reduce-scatter.2.cloned.1.call-done
  547.7 1.3 convert_element_type.3
  549.0 0.7 slice_bitcast_fusion.2
  549.7 1.0 slice_bitcast_fusion
  550.7 1.3 copy.28
  552.1 1.6 copy-done
  553.7 0.0 copy-start.8
  553.7 2.0 copy.29
  555.7 0.7 copy.30
  556.4 0.7 copy.31
  557.0 0.7 copy.32
  557.7 0.6 copy.33
  558.3 0.0 copy-done.8
  558.3 0.6 copy.34
  (19 shorter events, 0.1 us)
Async XLA Ops:
  7.2 99.4 %copy-start.7 = (bf16[1,512,64]{1,2,0:T(8,128)(2,1)S(1)}, bf16[1,512,64]{1,2,0:T(8,128)(2,1)}, u32[]{:S(2)}) copy-start(bf16[1,512,64]{1,2,0:T(8,128)(2,1)} %param.16) | copy-start | bytes 196612
  7.2 99.4 %copy-start.2 = (bf16[1,2048,64]{1,2,0:T(8,128)(2,1)S(1)}, bf16[1,2048,64]{1,2,0:T(8,128)(2,1)}, u32[]{:S(2)}) copy-start(bf16[1,2048,64]{1,2,0:T(8,128)(2,1)} %param.18) | copy-start | bytes 786436
  7.2 99.4 %copy-start.3 = (bf16[1,64,2048]{2,1,0:T(8,128)(2,1)S(1)}, bf16[1,64,2048]{2,1,0:T(8,128)(2,1)}, u32[]{:S(2)}) copy-start(bf16[1,64,2048]{2,1,0:T(8,128)(2,1)} %param.17) | copy-start | bytes 786436
  7.2 212.6 %all-gather.2.cloned.1.call-start = ((), (), s32[]{:S(2)}) async-start(), calls=%async_computation.2 | async-start | bytes 11141120 | tf_op jit(solution)/shard_map/all_gather | solution.py:1306
  7.3 99.3 %collective-permute-start = (bf16[64,512]{1,0:T(8,128)(2,1)}, bf16[64,512]{1,0:T(8,128)(2,1)S(1)}, u32[]{:S(2)}, u32[]{:S(2)}) collective-permute-start(bf16[64,512]{1,0:T(8,128)(2,1)} %bitcast.22), channel_id=1, source_target_pairs={{0,1},{1,0},{2,3},{3,2},{4,5},{5,4},{6,7},{7,6},{8,9},{9,8},{10,11... | collective-permute-start | bytes 196616 | tf_op jit(solution)/shard_map/ppermute | solution.py:1271
  10.3 97.4 %copy-start.10 = (s32[4]{0:T(128)S(1)}, s32[4]{0:T(128)}, u32[]{:S(2)}) copy-start(s32[4]{0:T(128)} %param.12) | copy-start | bytes 52
  107.6 440.2 %reduce-scatter.2.cloned.1.call-start = ((), (), s32[]{:S(2)}) async-start(), calls=%async_computation.3 | async-start | bytes 10027008 | tf_op jit(solution)/shard_map/reduce_scatter | solution.py:1318
  301.1 130.5 %collective-permute-start.1 = (bf16[1024,1024]{1,0:T(8,128)(2,1)}, bf16[1024,1024]{1,0:T(8,128)(2,1)}, u32[]{:S(2)}, u32[]{:S(2)}) collective-permute-start(bf16[1024,1024]{1,0:T(8,128)(2,1)} %get-tuple-element.48.z_far), channel_id=1, source_target_pairs={{0,1},{1,0},{2,3},{3,2},{4,5},{5,4},{6,7},{7,6},{8,9},{9,8},{10,11... | collective-permute-start | bytes 6291464 | tf_op jit(solution)/shard_map/ppermute | solution.py:1271
  547.7 3.0 copy-start.1
  550.7 2.9 copy-start
  553.7 2.0 copy-start.6
  553.7 2.7 copy-start.5
  553.7 3.4 copy-start.4
  553.7 4.0 copy-start.9
  553.7 4.6 copy-start.8
Sparse Core Ops, SparseCore 0:
  107.7 112.1 all-gather.1
  301.2 112.6 reduce-scatter.1
